TPU v7x, 32 devices: a whole 2x2x4 slice. The times are simulated.
32 devices in a mesh: dp: 8 (over z, y), mp: 4 (over x, core).
Axes of the slice: x: 2, y: 2, z: 4, core: 2. Of those that a mesh axis runs over, the one named last changes fastest.
Arguments:
- tokens: bfloat16 [16384, 1024], P(('dp', 'mp')), may hold values from -6 to 6
- lengths: int32 [16], P('dp'), may hold values from 256 to 1024, as said below
- norm1_gain: float32 [1024], replicated, may hold values from 0.5 to 1.5
- in_weight: bfloat16 [3, 1024, 1024], P(None, 'mp'), may hold values from -0.1875 to 0.1875
- conv_weight: bfloat16 [3, 1024], P(None, 'mp'), may hold values from -3.5 to 3.5
- out_weight: bfloat16 [1024, 1024], P('mp'), may hold values from -0.1875 to 0.1875
- norm2_gain: float32 [1024], replicated, may hold values from 0.5 to 1.5
- gate_weight: bfloat16 [4608, 1024], P('mp'), may hold values from -0.1875 to 0.1875
- up_weight: bfloat16 [4608, 1024], P('mp'), may hold values from -0.1875 to 0.1875
- down_weight: bfloat16 [4608, 1024], P('mp'), may hold values from -0.09375 to 0.09375
- cotangent: bfloat16 [16384, 1024], P(('dp', 'mp')), may hold values from -6 to 6
Outputs:
- block_out: bfloat16 [16384, 1024], P(('dp', 'mp'))
- tokens_grad: bfloat16 [16384, 1024], P(('dp', 'mp'))
- norm1_gain_grad: float32 [1024], replicated
- in_weight_grad: float32 [3, 1024, 1024], P(None, 'mp')
- conv_weight_grad: float32 [3, 1024], P(None, 'mp')
- out_weight_grad: float32 [1024, 1024], P('mp')
- norm2_gain_grad: float32 [1024], replicated
- gate_weight_grad: float32 [4608, 1024], P('mp')
- up_weight_grad: float32 [4608, 1024], P('mp')
- down_weight_grad: float32 [4608, 1024], P('mp')
Inputs may be any that keep to these rules, and one draw needn't show every extreme that they name: `lengths`: slots of a sequence past its length are padding; some sequence has all 1024 tokens and some has 256.
All inputs are finite; a program needn't handle non-finite values.
Results may differ from a plain program's by a relative error of at most 0.018.
Values may be sent and summed in bfloat16 or wider, within the bound.
A program may use at most 320 MiB of HBM per device.

v0:
```python
import jax
import jax.numpy as jnp
from jax import lax
from jax.sharding import PartitionSpec as P

SEQ_LEN = 1024


NORM_EPS = 1e-05
CONTRACT_ROWS = (((0,), (0,)), ((), ()))
CONTRACT_COLS = (((1,), (0,)), ((), ()))


def rms_scale(row_data):
    return lax.rsqrt(jnp.mean(row_data * row_data, axis=-1, keepdims=True) + NORM_EPS)


def rms_back(grad_scaled, row_data, scale_rows):
    inner_mean = jnp.mean(grad_scaled * row_data, axis=-1, keepdims=True)
    return scale_rows * grad_scaled - row_data * (scale_rows * scale_rows * scale_rows) * inner_mean


def row_layout(lengths, first_row, row_count):
    row_ids = first_row + jnp.arange(row_count, dtype=jnp.int32)
    positions = row_ids % SEQ_LEN
    owners = row_ids // SEQ_LEN
    seq_slots = jnp.arange(lengths.shape[0], dtype=jnp.int32)
    row_length = jnp.sum(
        jnp.where(owners[:, None] == seq_slots[None, :], lengths[None, :], 0), axis=1
    )
    return (positions, (positions < row_length).astype(jnp.float32))


def behind_last(values, steps_back, positions):
    pad_zeros = jnp.zeros(values.shape[:-1] + (steps_back,), values.dtype)
    moved_rows = jnp.concatenate([pad_zeros, values[..., :-steps_back]], axis=-1)
    return moved_rows * (positions >= steps_back).astype(values.dtype)


def ahead_last(values, steps_ahead, positions):
    kept_part = values * (positions >= steps_ahead).astype(values.dtype)
    pad_zeros = jnp.zeros(values.shape[:-1] + (steps_ahead,), values.dtype)
    return jnp.concatenate([kept_part[..., steps_ahead:], pad_zeros], axis=-1)


def split_forward(tokens, own_mask, row_positions, norm1_gain, norm2_gain, weight_set):
    in_weight, conv_weight, out_weight, gate_weight, up_weight, down_weight = weight_set
    x_rows = tokens.astype(jnp.float32)
    scale_one = rms_scale(x_rows)
    normed_one = (own_mask[:, None] * x_rows * scale_one * norm1_gain).astype(jnp.bfloat16)
    normed_one_all = lax.all_gather(normed_one, "mp", axis=0, tiled=True)
    projected = jnp.einsum(
        "kci,ti->kct", in_weight, normed_one_all, preferred_element_type=jnp.float32
    )
    conv_taps = conv_weight.astype(jnp.float32)
    mixed_bx = projected[0] * projected[2]
    one_back = behind_last(mixed_bx, 1, row_positions)
    two_back = behind_last(mixed_bx, 2, row_positions)
    convolved = (
        conv_taps[2][:, None] * mixed_bx
        + conv_taps[1][:, None] * one_back
        + conv_taps[0][:, None] * two_back
    )
    mixer_out = (projected[1] * convolved).astype(jnp.bfloat16)
    col_block = mixer_out
    hidden = x_rows + lax.psum_scatter(
        lax.dot_general(
            col_block, out_weight, CONTRACT_ROWS, preferred_element_type=jnp.float32
        ).astype(jnp.bfloat16),
        "mp",
        scatter_dimension=0,
        tiled=True,
    ).astype(jnp.float32)
    scale_two = rms_scale(hidden)
    normed_two = (hidden * scale_two * norm2_gain).astype(jnp.bfloat16)
    normed_two_all = lax.all_gather(normed_two, "mp", axis=0, tiled=True)
    gate_pre = jnp.einsum(
        "fi,ti->ft", gate_weight, normed_two_all, preferred_element_type=jnp.float32
    )
    up_pre = jnp.einsum("fi,ti->ft", up_weight, normed_two_all, preferred_element_type=jnp.float32)
    activ = (jax.nn.silu(gate_pre) * up_pre).astype(jnp.bfloat16)
    col_block = activ
    result = (
        hidden
        + lax.psum_scatter(
            lax.dot_general(
                col_block, down_weight, CONTRACT_ROWS, preferred_element_type=jnp.float32
            ).astype(jnp.bfloat16),
            "mp",
            scatter_dimension=0,
            tiled=True,
        ).astype(jnp.float32)
    ).astype(jnp.bfloat16)
    kept_state = (
        x_rows,
        scale_one,
        normed_one_all,
        projected,
        mixed_bx,
        one_back,
        two_back,
        convolved,
        mixer_out,
        hidden,
        scale_two,
        normed_two_all,
        gate_pre,
        up_pre,
        activ,
    )
    return (result, kept_state)


def split_backward(
    cotangent, own_mask, row_positions, kept_state, norm1_gain, norm2_gain, weight_set
):
    in_weight, conv_weight, out_weight, gate_weight, up_weight, down_weight = weight_set
    (
        x_rows,
        scale_one,
        normed_one_all,
        projected,
        mixed_bx,
        one_back,
        two_back,
        convolved,
        mixer_out,
        hidden,
        scale_two,
        normed_two_all,
        gate_pre,
        up_pre,
        activ,
    ) = kept_state
    grad_all = lax.all_gather(cotangent, "mp", axis=0, tiled=True)
    down_grad = lax.dot_general(activ, grad_all, CONTRACT_COLS, preferred_element_type=jnp.float32)
    grad_activ = jnp.einsum("fd,td->ft", down_weight, grad_all, preferred_element_type=jnp.float32)
    squash = jax.nn.sigmoid(gate_pre)
    grad_gate = (grad_activ * up_pre * squash * (1.0 + gate_pre * (1.0 - squash))).astype(
        jnp.bfloat16
    )
    grad_up = (grad_activ * gate_pre * squash).astype(jnp.bfloat16)
    gate_grad = lax.dot_general(
        grad_gate, normed_two_all, CONTRACT_COLS, preferred_element_type=jnp.float32
    )
    up_grad = lax.dot_general(
        grad_up, normed_two_all, CONTRACT_COLS, preferred_element_type=jnp.float32
    )
    grad_normed_two = lax.psum_scatter(
        (
            lax.dot_general(
                grad_gate, gate_weight, CONTRACT_ROWS, preferred_element_type=jnp.float32
            )
            + lax.dot_general(grad_up, up_weight, CONTRACT_ROWS, preferred_element_type=jnp.float32)
        ).astype(jnp.bfloat16),
        "mp",
        scatter_dimension=0,
        tiled=True,
    ).astype(jnp.float32)
    gain_two = jnp.sum(grad_normed_two * hidden * scale_two, axis=0)
    grad_hidden = cotangent.astype(jnp.float32) + rms_back(
        grad_normed_two * norm2_gain, hidden, scale_two
    )
    grad_branch = grad_hidden.astype(jnp.bfloat16)
    branch_all = lax.all_gather(grad_branch, "mp", axis=0, tiled=True)
    out_grad = lax.dot_general(
        mixer_out, branch_all, CONTRACT_COLS, preferred_element_type=jnp.float32
    )
    grad_mixer = jnp.einsum("cd,td->ct", out_weight, branch_all, preferred_element_type=jnp.float32)
    conv_taps = conv_weight.astype(jnp.float32)
    grad_conv = grad_mixer * projected[1]
    conv_grad = jnp.stack(
        [
            jnp.sum(grad_conv * two_back, axis=1),
            jnp.sum(grad_conv * one_back, axis=1),
            jnp.sum(grad_conv * mixed_bx, axis=1),
        ]
    )
    grad_mixed = (
        conv_taps[2][:, None] * grad_conv
        + conv_taps[1][:, None] * ahead_last(grad_conv, 1, row_positions)
        + conv_taps[0][:, None] * ahead_last(grad_conv, 2, row_positions)
    )
    grad_projected = jnp.stack(
        [grad_mixed * projected[2], grad_mixer * convolved, grad_mixed * projected[0]]
    ).astype(jnp.bfloat16)
    in_grad = jnp.einsum(
        "kct,ti->kci", grad_projected, normed_one_all, preferred_element_type=jnp.float32
    )
    grad_normed_one = lax.psum_scatter(
        jnp.einsum(
            "kct,kci->ti", grad_projected, in_weight, preferred_element_type=jnp.float32
        ).astype(jnp.bfloat16),
        "mp",
        scatter_dimension=0,
        tiled=True,
    ).astype(jnp.float32)
    masked_grad = own_mask[:, None] * grad_normed_one
    gain_one = jnp.sum(masked_grad * x_rows * scale_one, axis=0)
    grad_tokens = grad_hidden + rms_back(masked_grad * norm1_gain, x_rows, scale_one)
    weight_parts = (in_grad, conv_grad, out_grad, gate_grad, up_grad, down_grad)
    return (grad_tokens.astype(jnp.bfloat16), weight_parts, (gain_one, gain_two))


def on_device(
    tokens,
    lengths,
    norm1_gain,
    in_weight,
    conv_weight,
    out_weight,
    norm2_gain,
    gate_weight,
    up_weight,
    down_weight,
    cotangent,
):
    own_rows = tokens.shape[0]
    group_rows = own_rows * lax.axis_size("mp")
    own_positions, own_mask = row_layout(lengths, lax.axis_index("mp") * own_rows, own_rows)
    weight_set = (in_weight, conv_weight, out_weight, gate_weight, up_weight, down_weight)
    row_positions = jnp.arange(group_rows, dtype=jnp.int32) % SEQ_LEN

    def run_forward(row_data):
        return split_forward(row_data, own_mask, row_positions, norm1_gain, norm2_gain, weight_set)

    result, kept_state = run_forward(tokens)
    rows_again, grad_again = lax.optimization_barrier((tokens, cotangent))
    unused_out, kept_state = run_forward(rows_again)
    grad_tokens, weight_parts, gain_parts = split_backward(
        grad_again, own_mask, row_positions, kept_state, norm1_gain, norm2_gain, weight_set
    )
    weight_sums = (
        lax.psum(weight_parts[0].astype(jnp.bfloat16), "dp").astype(jnp.float32),
        lax.psum(weight_parts[1].astype(jnp.bfloat16), "dp").astype(jnp.float32),
        lax.psum(weight_parts[2].astype(jnp.bfloat16), "dp").astype(jnp.float32),
        lax.psum(weight_parts[3].astype(jnp.bfloat16), "dp").astype(jnp.float32),
        lax.psum(weight_parts[4].astype(jnp.bfloat16), "dp").astype(jnp.float32),
        lax.psum(weight_parts[5].astype(jnp.bfloat16), "dp").astype(jnp.float32),
    )
    gain_sums = lax.psum((gain_parts[0], gain_parts[1]), ("dp", "mp"))
    return (
        result,
        grad_tokens,
        gain_sums[0],
        weight_sums[0],
        weight_sums[1],
        weight_sums[2],
        gain_sums[1],
        weight_sums[3],
        weight_sums[4],
        weight_sums[5],
    )


def solution(mesh):
    placed = (
        P(("dp", "mp"), None),
        P("dp"),
        P(),
        P(None, "mp", None),
        P(None, "mp"),
        P("mp", None),
        P(),
        P("mp", None),
        P("mp", None),
        P("mp", None),
        P(("dp", "mp"), None),
    )
    return jax.shard_map(
        on_device,
        mesh=mesh,
        in_specs=placed,
        out_specs=(
            P(("dp", "mp"), None),
            P(("dp", "mp"), None),
            P(),
            P(None, "mp", None),
            P(None, "mp"),
            P("mp", None),
            P(),
            P("mp", None),
            P("mp", None),
            P("mp", None),
        ),
        check_vma=False,
    )
```

profile of v0, /device:TPU:0, one launch (start us, length us, event | category | flops | bytes accessed | tf_op | source)
XLA Modules:
  0.0 865.9 jit_solution(2118525626710275929)
XLA Ops:
  9.7 2.6 fusion.45
  12.4 37.2 %all-gather.11.cloned.1.call-done = bf16[2048,1024]{1,0:T(8,128)(2,1)} async-done(((bf16[512,1024]{1,0:T(8,128)(2,1)}), bf16[2048,1024]{1,0:T(8,128)(2,1)}) %all-gather.11.cloned.1.call-update) | async-done | bytes 4194320 | tf_op jit(solution)/shard_map/all_gather | solution.py:51
  49.6 5.7 fusion.26
  55.6 2.3 copy-done.3
  58.0 2.3 multiply_convert_fusion.4
  60.3 3.3 convolution_convert_fusion.2
  64.4 43.9 %reduce-scatter.10.cloned.1.call-done = bf16[512,1024]{1,0:T(8,128)(2,1)} async-done(((bf16[2048,1024]{1,0:T(8,128)(2,1)}), bf16[512,1024]{1,0:T(8,128)(2,1)}) %reduce-scatter.10.cloned.1.call-update) | async-done | bytes 1048592 | tf_op jit(solution)/shard_map/reduce_scatter | solution.py:66
  108.3 1.7 multiply_reduce_fusion.3
  111.7 32.7 %all-gather.13.cloned.1.call-done = bf16[2048,1024]{1,0:T(8,128)(2,1)} async-done(((bf16[512,1024]{1,0:T(8,128)(2,1)}), bf16[2048,1024]{1,0:T(8,128)(2,1)}) %all-gather.13.cloned.1.call-update) | async-done | bytes 4194320 | tf_op jit(solution)/shard_map/all_gather | solution.py:135
  144.4 10.2 %fusion.94 = f32[2048,1152]{1,0:T(8,128)} fusion(bf16[2048,1024]{1,0:T(8,128)(2,1)} %all-gather.13.cloned.1.call-done, bf16[1152,1024]{1,0:T(8,128)(2,1)} %param.20), kind=kOutput, calls=%fused_computation.155 | convolution fusion | flops 4831838208 | bytes 15990784 | tf_op jit(solution)/shard_map/fd,td->ft/dot_general | solution.py:137
  154.7 26.3 %all-gather.15.cloned.1.call-done = bf16[2048,1024]{1,0:T(8,128)(2,1)} async-done(((bf16[512,1024]{1,0:T(8,128)(2,1)}), bf16[2048,1024]{1,0:T(8,128)(2,1)}) %all-gather.15.cloned.1.call-update) | async-done | bytes 4194320 | tf_op jit(solution)/shard_map/all_gather | solution.py:76
  181.0 10.3 %fusion.95 = f32[2048,1152]{1,0:T(8,128)} fusion(bf16[2048,1024]{1,0:T(8,128)(2,1)} %all-gather.15.cloned.1.call-done, bf16[1152,1024]{1,0:T(8,128)(2,1)} %param.19), kind=kOutput, calls=%fused_computation.156 | convolution fusion | flops 4831838208 | bytes 15990784 | tf_op jit(solution)/shard_map/fi,ti->ft/dot_general | solution.py:80
  191.4 20.6 %fusion.7 = (bf16[1152,2048]{0,1:T(8,128)(2,1)}, bf16[1152,2048]{0,1:T(8,128)(2,1)}, f32[2048,1152]{1,0:T(8,128)}) fusion(f32[2048,1152]{1,0:T(8,128)} %fusion.94, f32[2048,1152]{1,0:T(8,128)} %fusion.95, bf16[2048,1024]{1,0:T(8,128)(2,1)} %all-gather.15.cloned.1.call-done, bf16[1152,1024]{1,0:T(8,128)(2,1)S(1)} %copy-done), kind=kOutput, calls=%fused_computation.11 | convolution fusion | flops 4862509056 | bytes 44302336 | tf_op jit(solution)/shard_map/fi,ti->ft/dot_general | solution.py:77
  211.9 7.6 fusion.96
  219.5 7.1 add_convert_fusion
  227.1 44.2 %reduce-scatter.12.cloned.1.call-done = bf16[512,1024]{1,0:T(8,128)(2,1)} async-done(((bf16[2048,1024]{1,0:T(8,128)(2,1)}), bf16[512,1024]{1,0:T(8,128)(2,1)}) %reduce-scatter.12.cloned.1.call-update) | async-done | bytes 1048592 | tf_op jit(solution)/shard_map/reduce_scatter | solution.py:149
  271.3 2.6 fusion.38
  273.9 1.8 fusion.90
  276.0 34.4 %all-gather.17.cloned.1.call-done = bf16[2048,1024]{1,0:T(8,128)(2,1)} async-done(((bf16[512,1024]{1,0:T(8,128)(2,1)}), bf16[2048,1024]{1,0:T(8,128)(2,1)}) %all-gather.17.cloned.1.call-update) | async-done | bytes 4194320 | tf_op jit(solution)/shard_map/all_gather | solution.py:165
  310.4 7.4 multiply_reduce_fusion.2
  318.6 2.4 fusion.63
  321.0 2.3 fusion.65
  324.2 4.9 bitcast_convert_fusion
  329.5 44.4 %reduce-scatter.14.cloned.1.call-done = bf16[512,1024]{1,0:T(8,128)(2,1)} async-done(((bf16[2048,1024]{1,0:T(8,128)(2,1)}), bf16[512,1024]{1,0:T(8,128)(2,1)}) %reduce-scatter.14.cloned.1.call-update) | async-done | bytes 1048592 | tf_op jit(solution)/shard_map/reduce_scatter | solution.py:190
  373.9 2.3 fusion.53
  376.3 4.0 fusion.50
  380.3 34.6 %all-gather.7.cloned.1.call-done = bf16[2048,1024]{1,0:T(8,128)(2,1)} async-done(((bf16[512,1024]{1,0:T(8,128)(2,1)}), bf16[2048,1024]{1,0:T(8,128)(2,1)}) %all-gather.7.cloned.1.call-update) | async-done | bytes 4194320 | tf_op jit(solution)/shard_map/all_gather | solution.py:51
  414.9 5.7 fusion.23
  421.7 3.6 convolution_convert_fusion.4
  425.5 44.5 %reduce-scatter.6.cloned.1.call-done = bf16[512,1024]{1,0:T(8,128)(2,1)} async-done(((bf16[2048,1024]{1,0:T(8,128)(2,1)}), bf16[512,1024]{1,0:T(8,128)(2,1)}) %reduce-scatter.6.cloned.1.call-update) | async-done | bytes 1048592 | tf_op jit(solution)/shard_map/reduce_scatter | solution.py:66
  469.9 1.7 multiply_reduce_fusion.4
  473.1 9.5 %convolution_convert_fusion = bf16[1152,1024]{1,0:T(8,128)(2,1)} fusion(bf16[1152,2048]{0,1:T(8,128)(2,1)} %get-tuple-element.33, bf16[2048,1024]{1,0:T(8,128)(2,1)} %all-gather.15.cloned.1.call-done), kind=kOutput, calls=%fused_computation.41 | convolution fusion | flops 4833017856 | bytes 11272192 | tf_op jit(solution)/shard_map/dot_general | solution.py:146
  482.6 8.8 %convolution_convert_fusion.1 = bf16[1152,1024]{1,0:T(8,128)(2,1)} fusion(bf16[1152,2048]{0,1:T(8,128)(2,1)} %get-tuple-element.34, bf16[2048,1024]{1,0:T(8,128)(2,1)S(1)} %copy-done.31), kind=kOutput, calls=%fused_computation.42 | convolution fusion | flops 4833017856 | bytes 11272192 | tf_op jit(solution)/shard_map/dot_general | solution.py:143
  491.4 11.8 %fusion.29 = bf16[1152,1024]{1,0:T(8,128)(2,1)} fusion(bf16[2048,1024]{1,0:T(8,128)(2,1)S(1)} %copy-done.30, f32[2048,1152]{1,0:T(8,128)} %get-tuple-element.45, f32[2048,1152]{1,0:T(8,128)} %fusion.95), kind=kOutput, calls=%fused_computation.40 | convolution fusion | flops 4847173632 | bytes 25427968 | tf_op jit(solution)/shard_map/dot_general | solution.py:136
  503.3 2.1 convolution_convert_fusion.5
  506.7 4.6 fusion.60
  511.6 9.7 %fusion.93 = f32[2048,1152]{1,0:T(8,128)} fusion(bf16[2048,1024]{1,0:T(8,128)(2,1)} %all-gather.9.cloned.1.call-done, bf16[1152,1024]{1,0:T(8,128)(2,1)S(1)} %copy-done), kind=kOutput, calls=%fused_computation.154 | convolution fusion | flops 4831838208 | bytes 15990784 | tf_op jit(solution)/shard_map/fi,ti->ft/dot_general | solution.py:77
  521.3 17.1 %convolution_convert_fusion.3 = bf16[2048,1024]{1,0:T(8,128)(2,1)} fusion(bf16[1152,1024]{1,0:T(8,128)(2,1)} %param.20, f32[2048,1152]{1,0:T(8,128)} %fusion.93, bf16[2048,1024]{1,0:T(8,128)(2,1)} %all-gather.9.cloned.1.call-done, bf16[1152,1024]{1,0:T(8,128)(2,1)} %param.19), kind=kOutput, calls=%fused_computation.44 | convolution fusion | flops 9679929344 | bytes 22544384 | tf_op jit(solution)/shard_map/dot_general | solution.py:86
  538.5 23.0 %psum.58 = bf16[3,256]{1,0:T(4,128)(2,1)S(1)} all-reduce(bf16[3,256]{1,0:T(4,128)(2,1)S(1)} %pad_maximum_fusion.3), channel_id=1, replica_groups=mesh['dp'=8,'mp'=4] {'dp'}, use_global_device_ids=true, to_apply=%region_18.19 | all-reduce | flops 768 | bytes 3072 | tf_op jit(solution)/shard_map/psum | solution.py:235
  562.0 40.1 %all-reduce.6 = (f32[1024]{0:T(1024)}, f32[1024]{0:T(1024)}) all-reduce(f32[1024]{0:T(1024)S(1)} %get-tuple-element.16, f32[1024]{0:T(1024)S(1)} %get-tuple-element.14), channel_id=1, replica_groups=mesh['dp'=8,'mp'=4] {'dp','mp'}, use_global_device_ids=true, to_apply=%region_13.14 | all-reduce | flops 2048 | bytes 16384 | tf_op jit(solution)/shard_map/psum | solution.py:241
  602.1 207.9 %all-reduce.10.cloned.1.call-done = (bf16[3,256,1024]{2,1,0:T(8,128)(2,1)}, bf16[256,1024]{1,0:T(8,128)(2,1)}, bf16[1152,1024]{1,0:T(8,128)(2,1)}, bf16[1152,1024]{1,0:T(8,128)(2,1)}, bf16[1152,1024]{1,0:T(8,128)(2,1)}) async-done(((bf16[3,256,1024]{2,1,0:T(8,128)(2,1)}, bf16[256,1024]{1,0:T(8,128)(2,1)}, bf16[1152,1024]{1,0:T(8,128)(2,1)}, bf16[1152,1024]{1,0:T(8,128)(2,1)}, bf16[1152,1024]{1,0:T(8,128)(2,1)}), ...) | async-done | bytes 9175056 | tf_op jit(solution)/shard_map/psum | solution.py:234
  810.0 2.2 convert_element_type.184
  812.3 2.1 convert_element_type.181
  814.7 2.9 convert_element_type.186
  817.6 3.1 convert_element_type.188
  820.7 2.7 convert_element_type.191
  823.4 32.3 %reduce-scatter.8.cloned.1.call-done = bf16[512,1024]{1,0:T(8,128)(2,1)} async-done(((bf16[2048,1024]{1,0:T(8,128)(2,1)}), bf16[512,1024]{1,0:T(8,128)(2,1)}) %reduce-scatter.8.cloned.1.call-update) | async-done | bytes 1048592 | tf_op jit(solution)/shard_map/reduce_scatter | solution.py:85
  855.7 3.1 add_convert_fusion.1
  (120 shorter events, 13.4 us)
Async XLA Ops:
  7.2 184.2 %copy-start = (bf16[1152,1024]{1,0:T(8,128)(2,1)S(1)}, bf16[1152,1024]{1,0:T(8,128)(2,1)}, u32[]{:S(2)}) copy-start(bf16[1152,1024]{1,0:T(8,128)(2,1)} %param.18) | copy-start | bytes 7077892
  7.2 42.4 %all-gather.11.cloned.1.call-start = ((), (), s32[]{:S(2)}) async-start(), calls=%async_computation.9 | async-start | bytes 5242880 | tf_op jit(solution)/shard_map/all_gather | solution.py:51
  7.2 5.1 copy-start.28
  12.3 96.0 %reduce-scatter.10.cloned.1.call-start = ((), (), s32[]{:S(2)}) async-start(), calls=%async_computation.10 | async-start | bytes 5242880 | tf_op jit(solution)/shard_map/reduce_scatter | solution.py:66
  55.3 2.6 copy-start.3
  55.6 4.7 copy-start.2
  58.0 2.3 copy-start.13
  60.3 3.3 copy-start.11
  63.6 44.7 %copy-start.1 = (bf16[512,1024]{1,0:T(8,128)(2,1)S(1)}, bf16[512,1024]{1,0:T(8,128)(2,1)}, u32[]{:S(2)}) copy-start(bf16[512,1024]{1,0:T(8,128)(2,1)} %param.11) | copy-start | bytes 3145732
  63.6 46.4 %copy-start.26 = (f32[1024]{0:T(1024)S(1)}, f32[1024]{0:T(1024)}, u32[]{:S(2)}) copy-start(f32[1024]{0:T(1024)} %param.17) | copy-start | bytes 12292
  63.6 80.8 %all-gather.13.cloned.1.call-start = ((), (), s32[]{:S(2)}) async-start(), calls=%async_computation.11 | async-start | bytes 5242880 | tf_op jit(solution)/shard_map/all_gather | solution.py:135
  64.4 116.7 %all-gather.15.cloned.1.call-start = ((), (), s32[]{:S(2)}) async-start(), calls=%async_computation.12 | async-start | bytes 5242880 | tf_op jit(solution)/shard_map/all_gather | solution.py:76
  108.3 1.8 copy-start.4
  111.5 159.9 %reduce-scatter.12.cloned.1.call-start = ((), (), s32[]{:S(2)}) async-start(), calls=%async_computation.13 | async-start | bytes 5242880 | tf_op jit(solution)/shard_map/reduce_scatter | solution.py:149
  211.9 7.6 copy-start.32
  211.9 7.6 copy-start.34
  226.6 83.8 %all-gather.17.cloned.1.call-start = ((), (), s32[]{:S(2)}) async-start(), calls=%async_computation.14 | async-start | bytes 5242880 | tf_op jit(solution)/shard_map/all_gather | solution.py:165
  271.3 2.6 copy-start.5
  271.3 2.6 copy-start.7
  271.3 2.6 copy-start.9
  275.8 98.1 %reduce-scatter.14.cloned.1.call-start = ((), (), s32[]{:S(2)}) async-start(), calls=%async_computation.15 | async-start | bytes 5242880 | tf_op jit(solution)/shard_map/reduce_scatter | solution.py:190
  317.9 5.4 copy-start.20
  321.0 2.3 copy-start.22
  321.0 3.3 copy-start.33
  323.3 1.0 copy-start.24
  329.2 44.7 %copy-start.27 = (f32[1024]{0:T(1024)S(1)}, f32[1024]{0:T(1024)}, u32[]{:S(2)}) copy-start(f32[1024]{0:T(1024)} %param.13) | copy-start | bytes 12292
  329.2 85.7 %all-gather.7.cloned.1.call-start = ((), (), s32[]{:S(2)}) async-start(), calls=%async_computation.5 | async-start | bytes 5242880 | tf_op jit(solution)/shard_map/all_gather | solution.py:51
  373.9 2.3 copy-start.6
  373.9 2.3 copy-start.8
  380.2 89.7 %reduce-scatter.6.cloned.1.call-start = ((), (), s32[]{:S(2)}) async-start(), calls=%async_computation.6 | async-start | bytes 5242880 | tf_op jit(solution)/shard_map/reduce_scatter | solution.py:66
  420.6 1.0 copy-start.14
  425.2 86.3 %all-gather.9.cloned.1.call-start = ((), (), s32[]{:S(2)}) async-start(), calls=%async_computation.7 | async-start | bytes 5242880 | tf_op jit(solution)/shard_map/all_gather | solution.py:76
  469.9 1.7 copy-start.10
  473.1 336.9 %all-reduce.10.cloned.1.call-start = ((), (), s32[]{:S(2)}) async-start(), calls=%async_computation.16 | async-start | bytes 18350080 | tf_op jit(solution)/shard_map/psum | solution.py:234
  473.1 9.5 %copy-start.31 = (bf16[2048,1024]{1,0:T(8,128)(2,1)S(1)}, bf16[2048,1024]{1,0:T(8,128)(2,1)}, u32[]{:S(2)}) copy-start(bf16[2048,1024]{1,0:T(8,128)(2,1)} %all-gather.15.cloned.1.call-done) | copy-start | bytes 12582916
  482.6 8.9 %copy-start.30 = (bf16[2048,1024]{1,0:T(8,128)(2,1)S(1)}, bf16[2048,1024]{1,0:T(8,128)(2,1)}, u32[]{:S(2)}) copy-start(bf16[2048,1024]{1,0:T(8,128)(2,1)} %all-gather.13.cloned.1.call-done) | copy-start | bytes 12582916
  491.4 11.8 %copy-start.12 = (bf16[256,2048]{0,1:T(8,128)(2,1)S(1)}, bf16[256,2048]{0,1:T(8,128)(2,1)}, u32[]{:S(2)}) copy-start(bf16[256,2048]{0,1:T(8,128)(2,1)} %copy-done.11) | copy-start | bytes 3145732
  491.4 11.8 %copy-start.15 = (bf16[2048,1024]{1,0:T(8,128)(2,1)S(1)}, bf16[2048,1024]{1,0:T(8,128)(2,1)}, u32[]{:S(2)}) copy-start(bf16[2048,1024]{1,0:T(8,128)(2,1)} %all-gather.17.cloned.1.call-done) | copy-start | bytes 12582916
  503.3 2.1 copy-start.21
  503.3 2.1 copy-start.23
  503.3 2.1 copy-start.25
  503.3 3.4 copy-start.29
  511.3 344.4 %reduce-scatter.8.cloned.1.call-start = ((), (), s32[]{:S(2)}) async-start(), calls=%async_computation.8 | async-start | bytes 5242880 | tf_op jit(solution)/shard_map/reduce_scatter | solution.py:85
  810.0 2.2 copy-start.19
  812.2 2.4 copy-start.18
  814.7 2.9 copy-start.17
  817.6 3.1 copy-start.16
Sparse Core Ops, SparseCore 0:
  12.4 37.1 all-gather.10
  63.7 44.4 reduce-scatter.9
  109.9 34.4 all-gather.12
  146.5 34.4 all-gather.14
  226.8 44.5 reduce-scatter.11
  275.9 34.4 all-gather.16
  329.3 44.5 reduce-scatter.13
  380.4 34.4 all-gather.6
  425.4 44.5 reduce-scatter.5
  473.2 34.4 all-gather.8
  513.9 296.0 all-reduce.9
  812.4 43.2 reduce-scatter.7
where the time goes:
time: 871 us; the launch traced here: 866 us
  waiting for transfers between devices  583 us (67%)
  matrix products  150 us (17%)
  blocking collectives  63 us (7%)
  other arithmetic  47.3 us (5%)
  between operations  14.8 us (2%)
    psum x1, waiting for transfers between devices, on_device(): lax.psum(weight_parts[0].astype(jnp.bfloat16), 'dp').astype(jnp.float32)  208 us
    reduce_scatter x2, waiting for transfers between devices, split_forward(): lax.psum_scatter(lax.dot_general(col_block, out_weight, CONTRACT_ROWS, pr...  88.3 us
    all_gather x2, waiting for transfers between devices, split_forward(): normed_one_all = lax.all_gather(normed_one, 'mp', axis=0, tiled=True)  71.8 us
    reduce_scatter x1, waiting for transfers between devices, split_backward(): lax.psum_scatter(jnp.einsum('kct,kci->ti', grad_projected, in_weight, pre...  44.4 us
    reduce_scatter x1, waiting for transfers between devices, split_backward(): lax.psum_scatter((lax.dot_general(grad_gate, gate_weight, CONTRACT_ROWS,...  44.2 us
    psum x1, blocking collectives, on_device(): gain_sums = lax.psum((gain_parts[0], gain_parts[1]), ('dp', 'mp'))  40.1 us
    all_gather x1, waiting for transfers between devices, split_backward(): branch_all = lax.all_gather(grad_branch, 'mp', axis=0, tiled=True)  34.4 us
    all_gather x1, waiting for transfers between devices, split_backward(): grad_all = lax.all_gather(cotangent, 'mp', axis=0, tiled=True)  32.7 us
  transfers between devices with their start and end apart: 12, of which 11 were waited for; matrix products, arithmetic and copies ran while one was open for 11% of the time, Pallas kernels for 0%

commit v1 on v0

v1 whole, which is shorter than its diff:
```python
import functools

import jax
import jax.numpy as jnp
from jax import lax
from jax.experimental import pallas as pl
from jax.experimental.pallas import tpu as pltpu
from jax.sharding import PartitionSpec as P

SEQ_LEN = 1024
NORM_EPS = 1e-05
F32 = jnp.float32
BF16 = jnp.bfloat16
MESH = pl.DeviceIdType.MESH
LANES = 128


def rms_scale(row_data):
    return lax.rsqrt(jnp.mean(row_data * row_data, axis=-1, keepdims=True) + NORM_EPS)


def rms_back(grad_scaled, row_data, scale_rows):
    inner_mean = jnp.mean(grad_scaled * row_data, axis=-1, keepdims=True)
    return scale_rows * grad_scaled - row_data * (scale_rows * scale_rows * scale_rows) * inner_mean


def dot(left, right, left_dim, right_dim):
    return lax.dot_general(
        left, right, (((left_dim,), (right_dim,)), ((), ())), preferred_element_type=F32
    )


def to_partner(values):
    count = lax.axis_size("mp")
    return lax.ppermute(values, "mp", [(i, i ^ 1) for i in range(count)])


def to_chip(values, ahead):
    count = lax.axis_size("mp")
    return lax.ppermute(values, "mp", [(i, (i + 2 * ahead) % count) for i in range(count)])


def gather_rows(own):
    chips = lax.axis_size("mp") // 2
    first = lax.axis_index("mp") % 2 == 0
    mine = [own] + [to_chip(own, chips - r) for r in range(1, chips)]
    blocks = []
    for block in mine:
        other = to_partner(block)
        blocks += [jnp.where(first, block, other), jnp.where(first, other, block)]
    return jnp.concatenate(blocks, axis=0)


def scatter_sum(partial, own_rows):
    chips = lax.axis_size("mp") // 2
    first = lax.axis_index("mp") % 2 == 0
    blocks = partial.reshape(chips, 2, own_rows, partial.shape[-1])
    sums = []
    for r in range(chips):
        theirs = to_partner(jnp.where(first, blocks[r, 1], blocks[r, 0]))
        mine = jnp.where(first, blocks[r, 0], blocks[r, 1])
        sums.append(mine.astype(F32) + theirs.astype(F32))
    total = sums[0]
    for r in range(1, chips):
        total = total + to_chip(sums[r].astype(BF16), r).astype(F32)
    return total


def ring_place(device, count):
    z, y = device // 2, device % 2
    return y * (count - 1 - z) + (1 - y) * z


def ring_device(place, count):
    back = place // (count // 2)
    return (1 - back) * 2 * place + back * (2 * (count - 1 - place) + 1)


def ring_sum(pieces):
    count = lax.axis_size("dp")
    order = [ring_device(i, count) for i in range(count)]
    place = ring_place(lax.axis_index("dp"), count)
    right = [(order[i], order[(i + 1) % count]) for i in range(count)]
    left = [(b, a) for a, b in right]

    def take(source, half, index):
        return lax.dynamic_index_in_dim(source, half * count + index, 0, keepdims=False)

    total = jnp.zeros(pieces.shape, BF16)
    moving = [take(pieces, 0, place), take(pieces, 1, place)]
    for step in range(1, count):
        moving = [lax.ppermute(moving[0], "dp", right), lax.ppermute(moving[1], "dp", left)]
        at = [(place - step + count) % count, (place + step) % count]
        moving = [
            (moving[h].astype(F32) + take(pieces, h, at[h]).astype(F32)).astype(BF16)
            for h in range(2)
        ]
    at = [(place + 1) % count, (place - 1 + count) % count]
    for h in range(2):
        total = lax.dynamic_update_index_in_dim(total, moving[h], h * count + at[h], 0)
    for step in range(1, count):
        moving = [lax.ppermute(moving[0], "dp", right), lax.ppermute(moving[1], "dp", left)]
        at = [(place + 1 - step + count) % count, (place - 1 + step) % count]
        for h in range(2):
            total = lax.dynamic_update_index_in_dim(total, moving[h], h * count + at[h], 0)
    return total


def sum_weights(parts):
    count = 2 * lax.axis_size("dp")
    stacked = jnp.concatenate(
        [part.astype(BF16).reshape(count, part.shape[0] // count, part.shape[1]) for part in parts],
        axis=1,
    )
    total = ring_sum(stacked)
    results = []
    at = 0
    for part in parts:
        rows = part.shape[0] // count
        results.append(total[:, at : at + rows].reshape(part.shape).astype(F32))
        at += rows
    return results


def butterfly(values, axis):
    count = lax.axis_size(axis)
    step = 1
    while step < count:
        values = values + lax.ppermute(values, axis, [(i, i ^ step) for i in range(count)])
        step *= 2
    return values


def block_by_ops(
    tokens,
    lengths,
    norm1_gain,
    in_weight,
    conv_weight,
    out_weight,
    norm2_gain,
    gate_weight,
    up_weight,
    down_weight,
    cotangent,
):
    own_rows, width = tokens.shape
    chips = lax.axis_size("mp") // 2
    chip = lax.axis_index("mp") // 2
    core = lax.axis_index("mp") % 2
    positions = core * own_rows + jnp.arange(own_rows, dtype=jnp.int32)
    seq_slots = jnp.arange(lengths.shape[0], dtype=jnp.int32)
    own_length = jnp.sum(jnp.where(seq_slots == chip, lengths, 0))
    own_mask = (positions < own_length).astype(F32)[:, None]
    channels = in_weight.shape[1]
    group_rows = 2 * chips * own_rows
    x_rows = tokens.astype(F32)
    scale_one = rms_scale(x_rows)
    normed_one = (own_mask * x_rows * scale_one * norm1_gain).astype(BF16)
    normed_one_all = gather_rows(normed_one)
    proj, shifted, conv, mixer_out = mixer_forward(normed_one_all, in_weight, conv_weight, chips)
    branch = scatter_sum(dot(mixer_out, out_weight, 1, 0).astype(BF16), own_rows)
    hidden = x_rows + branch
    scale_two = rms_scale(hidden)
    normed_two = (hidden * scale_two * norm2_gain).astype(BF16)
    normed_two_all = gather_rows(normed_two)
    cot_all = gather_rows(cotangent)
    gate_pre = dot(normed_two_all, gate_weight, 1, 1)
    up_pre = dot(normed_two_all, up_weight, 1, 1)
    squash = jax.nn.sigmoid(gate_pre)
    activ = (gate_pre * squash * up_pre).astype(BF16)
    grad_activ = dot(cot_all, down_weight, 1, 1)
    grad_gate = (grad_activ * up_pre * squash * (1.0 + gate_pre * (1.0 - squash))).astype(BF16)
    grad_up = (grad_activ * gate_pre * squash).astype(BF16)
    down_grad = dot(activ, cot_all, 0, 0)
    gate_grad = dot(grad_gate, normed_two_all, 0, 0)
    up_grad = dot(grad_up, normed_two_all, 0, 0)
    down_grad, gate_grad, up_grad = sum_weights([down_grad, gate_grad, up_grad])

    grad_normed_two = scatter_sum(
        (dot(grad_gate, gate_weight, 1, 0) + dot(grad_up, up_weight, 1, 0)).astype(BF16), own_rows
    )
    gain_two = jnp.sum(grad_normed_two * hidden * scale_two, axis=0)
    grad_hidden = cotangent.astype(F32) + rms_back(grad_normed_two * norm2_gain, hidden, scale_two)
    branch_all = gather_rows(grad_hidden.astype(BF16))
    taps = conv_weight.astype(F32)
    out_grad = dot(mixer_out, branch_all, 0, 0)
    grad_mixer = dot(branch_all, out_weight, 1, 1).reshape(chips, 2 * own_rows, channels)
    grad_conv = grad_mixer * proj[1]
    conv_grad = jnp.stack([jnp.sum(grad_conv * shifted[k], axis=(0, 1)) for k in range(3)])
    grad_pad = jnp.pad(grad_conv, ((0, 0), (0, 2), (0, 0)))
    grad_mixed = (
        taps[2] * grad_conv
        + taps[1] * grad_pad[:, 1 : 1 + 2 * own_rows]
        + taps[0] * grad_pad[:, 2 : 2 + 2 * own_rows]
    )
    grad_proj = [
        piece.astype(BF16).reshape(group_rows, channels)
        for piece in (grad_mixed * proj[2], grad_mixer * conv, grad_mixed * proj[0])
    ]
    in_grad = [dot(piece, normed_one_all, 0, 0) for piece in grad_proj]
    in_grad_0, in_grad_1, in_grad_2, out_grad = sum_weights(in_grad + [out_grad])
    grad_normed_one = scatter_sum(
        sum(dot(grad_proj[k], in_weight[k], 1, 0) for k in range(3)).astype(BF16), own_rows
    )
    masked_grad = own_mask * grad_normed_one
    gain_one = jnp.sum(masked_grad * x_rows * scale_one, axis=0)
    grad_tokens = grad_hidden + rms_back(masked_grad * norm1_gain, x_rows, scale_one)
    gains = butterfly(jnp.concatenate([gain_one, gain_two]), "mp")
    small = butterfly(jnp.concatenate([gains, conv_grad.reshape(-1)]), "dp")
    result = hidden + scatter_sum(dot(activ, down_weight, 1, 0).astype(BF16), own_rows)
    return (
        result.astype(BF16),
        grad_tokens.astype(BF16),
        small[:width],
        jnp.stack([in_grad_0, in_grad_1, in_grad_2]),
        small[2 * width :].reshape(3, channels),
        out_grad,
        small[width : 2 * width],
        gate_grad,
        up_grad,
        down_grad,
    )


def mixer_forward(normed_one_all, in_weight, conv_weight, chips):
    rows = normed_one_all.shape[0] // chips
    channels = in_weight.shape[1]
    proj = [dot(normed_one_all, in_weight[k], 1, 1).reshape(chips, rows, channels) for k in range(3)]
    taps = conv_weight.astype(F32)
    mixed_pad = jnp.pad(proj[0] * proj[2], ((0, 0), (2, 0), (0, 0)))
    shifted = [mixed_pad[:, k : k + rows] for k in range(3)]
    conv = taps[0] * shifted[0] + taps[1] * shifted[1] + taps[2] * shifted[2]
    mixer_out = (proj[1] * conv).astype(BF16).reshape(chips * rows, channels)
    return proj, shifted, conv, mixer_out


CHUNKS = 3
TILE = 256
KINDS = (
    ("A1", "PF1", "PF2", "PF3", "PG1", "PG2", "PG3")
    + ("QF1", "QF2", "QF3", "QSW", "QG1", "QG2", "QG3")
)
AT_END = (
    (),
    (),
    (0,),
    (100,),
    (),
    (9,),
    (200,),
    (109, 300),
    (3, 10),
    (110, 209),
    (),
    (309, 103),
    (210, 203),
    (),
    (),
    (303, 400, 6),
    (),
    (500, 13),
    (310,),
    (113,),
    (409, 509),
    (),
    (),
    (106,),
    (410, 213, 510),
    (206,),
    (),
    (306,),
    (),
    (403,),
    (),
    (),
    (600, 503),
    (313,),
    (700,),
    (800, 413),
    (900, 513, 609, 709, 809, 610, 909, 710, 603, 810, 406, 910, 703),
    (803, 903, 506, 613),
    (),
    (713,),
    (),
    (606,),
    (813, 913, 706, 806, 906),
)
INSIDE = (
    (),
    (7,),
    (0, 107, 8, 100),
    (),
    (1,),
    (108, 207),
    (200, 2, 307),
    (208, 101, 300, 201),
    (308, 301, 102),
    (4, 202, 11, 302),
    (111,),
    (5, 407),
    (12, 507),
    (),
    (),
    (400, 112, 104, 408),
    (211, 500, 204),
    (508,),
    (304, 105),
    (401,),
    (212, 501, 205, 311),
    (),
    (),
    (305, 402),
    (502, 312, 411),
    (),
    (),
    (511,),
    (412,),
    (607, 707),
    (807, 600, 512),
    (),
    (907, 608, 700, 708),
    (808, 601, 800, 908),
    (404,),
    (900, 602, 701, 504),
    (801, 405, 901, 702, 505, 611, 802, 711, 902, 604, 612, 811, 712, 911, 605, 704, 812),
    (912, 705, 804, 904),
    (),
    (),
    (805,),
    (905,),
    (),
)
CUT = 2
SLABS = 4
STRIP = 128
EDGE = 8


def block_kernel(
    count,
    tok_hbm,
    cot_hbm,
    gate_hbm,
    up_hbm,
    down_hbm,
    inw_hbm,
    outw_hbm,
    conv_ref,
    gain1,
    gain2,
    lengths,
    out_hbm,
    tg_hbm,
    gate_out,
    up_out,
    down_out,
    in_out,
    mix_out,
    small_out,
    n1_hbm,
    acts,
    wgu,
    wd,
    agu,
    aa,
    gf,
    land_a,
    land_p,
    land_q,
    gm,
    sa,
    ra,
    xr,
    wmix,
    f1,
    f2,
    taps,
    taps2,
    mbuf,
    gbuf,
    pbuf,
    smv,
    smb,
    ld_sem,
    ring_send,
    ring_recv,
    sum_send,
    sum_recv,
    half_free,
    rows_free,
    slots_free,
    mp_send,
    mp_recv,
    credit,
):
    own, width = out_hbm.shape
    group = 4 * own
    hidden_units = wd.shape[0]
    chunk = hidden_units // CHUNKS
    channels = outw_hbm.shape[0]
    per_block = own // TILE

    me_dp, me_mp = lax.axis_index("dp"), lax.axis_index("mp")
    core = me_mp % 2
    partner = (me_dp, me_mp + 1 - 2 * core)
    across = (me_dp, (me_mp + 2) % 4)
    place = ring_place(me_dp, count)
    nexts = [
        (ring_device((place + step) % count, count), me_mp) for step in (1, count - 1)
    ]
    signs = (1, -1)
    z, y = me_dp // 2, me_dp % 2
    side = z // 2
    inside = ((z + 1) // 2) % 2 == 1
    beside = (2 * z + 1 - y, me_mp)
    along = (2 * (z + 1 - 2 * (z % 2)) + y, me_mp)
    middle = (2 * (3 - z) + y, me_mp)
    opposite = (2 * ((z + 2) % 4) + y, me_mp)

    def rows_at(r, c):
        return pl.multiple_of((2 * r + c) * own, own)

    mine, theirs = core, 1 - core

    def load(src, dst, index):
        return pltpu.make_async_copy(src, dst, ld_sem.at[index])

    def weight_loads(c):
        at = pl.multiple_of(c * chunk, chunk)
        to = pl.multiple_of(2 * c * chunk, chunk)
        rows = pl.ds(at, chunk)
        return [
            load(gate_hbm.at[rows], wgu.at[pl.ds(to, chunk)], 3 * c),
            load(up_hbm.at[rows], wgu.at[pl.ds(to + chunk, chunk)], 3 * c + 1),
            load(down_hbm.at[rows], wd.at[rows], 3 * c + 2),
        ]

    def block_of(ref, r, c):
        return ref.at[pl.ds(rows_at(r, c), own)]

    inw = wmix.at[pl.ds(0, 3 * channels)]
    outw = wmix.at[pl.ds(3 * channels, channels)]
    late = 3 * CHUNKS
    inw_load = load(inw_hbm, inw, late)
    outw_load = load(outw_hbm, outw, late + 1)
    tok_load = load(tok_hbm, ra.at[1], late + 2)
    tok_again = load(tok_hbm, acts.at[0, pl.ds(0, own)], late + 2)
    cot_load = load(cot_hbm, block_of(acts.at[1], 0, mine), late + 3)
    n1_load = load(n1_hbm, acts.at[0, pl.ds(0, 2 * own)], late + 4)
    n1_move = load(gm.at[pl.ds(0, 2 * own)], acts.at[0, pl.ds(2 * own, 2 * own)], late + 9)
    out_store = load(sa.at[0], out_hbm, late + 5)
    tg_store = load(sa.at[1], tg_hbm, late + 6)
    n1_stores = [
        load(sa.at[c], n1_hbm.at[pl.ds(c * own, own)], late + 7 + c) for c in range(2)
    ]
    late += 10
    grad_stores = [
        load(
            gf.at[c, pl.ds(k * chunk, chunk)],
            ref.at[pl.ds(c * chunk, chunk)],
            late + CHUNKS * k + c,
        )
        for k, ref in enumerate((gate_out, up_out, down_out))
        for c in range(CHUNKS)
    ]
    late += 3 * CHUNKS
    mixer_stores = [
        load(gm.at[pl.ds(0, 3 * channels)], in_out, late),
        load(gm.at[pl.ds(3 * channels, channels)], mix_out, late + 1),
    ]

    for item in (inw_load, outw_load, cot_load, tok_load):
        item.start()
    for c in range(CHUNKS):
        for item in weight_loads(c):
            item.start()

    barrier = pltpu.get_barrier_semaphore()
    for device in (partner, across, beside, along, opposite):
        pl.semaphore_signal(barrier, inc=1, device_id=device, device_id_type=MESH)

    @pl.when(inside)
    def _():
        pl.semaphore_signal(barrier, inc=1, device_id=middle, device_id_type=MESH)
        pl.semaphore_wait(barrier, 6)

    @pl.when(jnp.logical_not(inside))
    def _():
        pl.semaphore_wait(barrier, 5)

    def ring_copy(src, dst, lane, h, number):
        return pltpu.make_async_remote_copy(
            src_ref=src,
            dst_ref=dst,
            send_sem=ring_send.at[lane, h, number],
            recv_sem=ring_recv.at[lane, h, number],
            device_id=nexts[h],
            device_id_type=MESH,
        )

    first = 5 * width // 8

    def make_part(bucket, start, rows, landing, number):
        quarter, two = rows // 4, rows // 2

        def own_half(h):
            at = pl.multiple_of(start + h * two, 16)
            return bucket.at[pl.ds(at, two), pl.ds(0, first)]

        def part_p(f):
            at = pl.multiple_of(start + y * two + f * quarter, 16)
            return bucket.at[pl.ds(at, quarter), pl.ds(0, first)]

        def part_q(f):
            at = pl.multiple_of(start + f * two, 16)
            return bucket.at[pl.ds(at, two), pl.ds(first, width - first)]

        def send(index, src, dst, device):
            return pltpu.make_async_remote_copy(
                src_ref=src,
                dst_ref=dst,
                send_sem=sum_send.at[number, index],
                recv_sem=sum_recv.at[number, index],
                device_id=device,
                device_id_type=MESH,
            )

        def arrived(index, ref):
            send(index, ref, ref, beside).wait_recv()

        def sent(index, ref):
            send(index, ref, ref, beside).wait_send()

        def add(target, ref):
            target[...] = target[...] + ref[...]

        land_a, land_p, land_q = landing
        ours, other = side, 1 - side
        a1, p1, p2, q1, q2, pg1, pg2, qg1, qg2, ya, yb = range(11)

        def half_sum(f):
            return land_a.at[pl.ds(pl.multiple_of(f * quarter, 16), quarter)]

        def begin():
            send(a1, own_half(1 - y), land_a, beside).start()

            @pl.when(jnp.logical_not(inside))
            def _():
                send(q1, part_q(ours), land_q[0], along).start()

        told = set()

        def hand_over(index, f, at_end):
            if at_end not in told:
                told.add(at_end)
                pl.semaphore_wait(half_free.at[number], 1)
            send(index, part_p(f), part_p(f), beside).start()

        def sum_rows(kind, at_end):
            if kind == "A1":
                arrived(a1, land_a)
                add(land_a, own_half(y))
                if at_end:
                    send(p1, half_sum(ours), land_p[0], along).start()
                sent(a1, land_a)
                pl.semaphore_signal(
                    half_free.at[number], inc=1, device_id=beside, device_id_type=MESH
                )
            elif kind == "PF1":
                arrived(p1, land_p[0])
                add(land_p[0], half_sum(ours))
                send(p2, land_p[0], land_p[1], middle).start()
            elif kind == "PF2":
                arrived(p2, land_p[1])
                add(land_p[1], half_sum(other))
                send(p1, land_p[1], land_p[0], along).start()
            elif kind == "PF3":
                arrived(p1, land_p[0])
                part_p(other)[...] = land_p[0][...] + half_sum(other)[...]
                send(pg1, part_p(other), part_p(other), along).start()
                hand_over(ya, other, at_end)
            elif kind == "PG1":
                arrived(pg1, part_p(other))
                send(pg2, part_p(other), part_p(other), middle).start()
                hand_over(ya, other, at_end)
            elif kind == "PG2":
                arrived(pg2, part_p(ours))
                send(pg1, part_p(ours), part_p(ours), along).start()
                hand_over(yb, ours, at_end)
            elif kind == "PG3":
                arrived(pg1, part_p(ours))
                hand_over(yb, ours, at_end)
            elif kind == "QF1":
                arrived(q1, land_q[0])
                add(land_q[0], part_q(ours))
                send(q2, land_q[0], land_q[1], middle).start()
            elif kind == "QF2":
                arrived(q2, land_q[1])
                add(land_q[1], part_q(other))
                send(q1, land_q[1], land_q[0], along).start()
            elif kind == "QF3":
                arrived(q1, land_q[0])
                add(land_q[0], part_q(other))
                send(q2, land_q[0], land_q[1], beside).start()
                sent(q1, land_q[0])
                pl.semaphore_signal(
                    rows_free.at[number], inc=1, device_id=along, device_id_type=MESH
                )
            elif kind == "QSW":
                arrived(q2, land_q[1])
                part_q(other)[...] = land_q[0][...] + land_q[1][...]
                send(qg1, part_q(other), part_q(other), along).start()
            elif kind == "QG1":
                arrived(qg1, part_q(other))
                send(qg2, part_q(other), part_q(other), middle).start()
            elif kind == "QG2":
                arrived(qg2, part_q(ours))
                pl.semaphore_wait(rows_free.at[number], 1)
                send(qg1, part_q(ours), part_q(ours), along).start()
            elif kind == "QG3":
                arrived(qg1, part_q(ours))

        def end():
            for index, f in ((ya, other), (yb, ours)):
                at = pl.multiple_of(start + (1 - y) * two + f * quarter, 16)
                arrived(index, bucket.at[pl.ds(at, quarter), pl.ds(0, first)])
            for index in (p1, pg1, ya, yb):
                sent(index, part_p(0))
            for index in (q2, qg1):
                sent(index, part_q(0))

            @pl.when(inside)
            def _():
                for index in (p2, pg2):
                    sent(index, part_p(0))
                for index in (q1, qg2):
                    sent(index, part_q(0))

        return begin, sum_rows, end

    part_rows, slab_rows = 3 * chunk // CUT, 4 * channels // SLABS
    parts_list = []
    for c in range(CHUNKS):
        for k in range(CUT):
            slot = CUT * c + k
            landing = (
                land_a.at[slot],
                [land_p.at[slot, 0], land_p.at[slot, 1]],
                [land_q.at[slot, 0], land_q.at[slot, 1]],
            )
            parts_list.append(make_part(gf.at[c], k * part_rows, part_rows, landing, slot))
    for k in range(SLABS):
        slot, upper = k // 2, k % 2
        two, quarter = slab_rows // 2, slab_rows // 4
        landing = (
            land_a.at[slot, pl.ds(upper * two, two)],
            [land_p.at[slot, i, pl.ds(upper * quarter, quarter)] for i in range(2)],
            [land_q.at[slot, i, pl.ds(upper * two, two)] for i in range(2)],
        )
        parts_list.append(
            make_part(gm, k * slab_rows, slab_rows, landing, CUT * CHUNKS + k)
        )

    def sum_start(c):
        chosen = range(CUT * c, CUT * c + CUT) if c < CHUNKS else range(CUT * c, len(parts_list))
        for number in chosen:
            parts_list[number][0]()

    def chunk_end(c):
        for number in range(CUT * c, CUT * c + CUT):
            parts_list[number][2]()
        for item in grad_stores[c::CHUNKS]:
            item.start()

    sites = iter(zip(AT_END, INSIDE))

    def pump():
        at_end, within = next(sites)

        @pl.when(jnp.logical_not(inside))
        def _():
            for event in at_end:
                parts_list[event // 100][1](KINDS[event % 100], True)

        @pl.when(inside)
        def _():
            for event in within:
                parts_list[event // 100][1](KINDS[event % 100], False)

    def mp_copy(src, dst, device, number):
        return pltpu.make_async_remote_copy(
            src_ref=src,
            dst_ref=dst,
            send_sem=mp_send.at[number],
            recv_sem=mp_recv.at[number],
            device_id=device,
            device_id_type=MESH,
        )

    def block_tiles(r, c, body):
        @pl.loop(0, per_block)
        def _(t):
            at = pl.multiple_of(t * TILE, TILE)
            body(pl.ds(pl.multiple_of(rows_at(r, c) + at, TILE), TILE), pl.ds(at, TILE))

    def strips(body):
        @pl.loop(0, own // STRIP)
        def _(t):
            body(pl.ds(pl.multiple_of(t * STRIP, STRIP), STRIP))

    base_copy = 14 + count - 1
    halves = [pl.ds(h * (width // 2), width // 2) for h in range(2)]
    span = 3 * channels // count

    def piece_rows(index):
        return pl.ds(pl.multiple_of(index * span, 16), span)

    piece_copies = [
        mp_copy(
            wmix.at[piece_rows(place), cols],
            gm.at[piece_rows(place), cols],
            across,
            base_copy + h,
        )
        for h, cols in enumerate(halves)
    ]
    outw_far = gm.at[pl.ds(3 * channels, channels)]
    outw_copy = mp_copy(outw, outw_far, across, base_copy + 11 + 3 * per_block)
    taps_copy = mp_copy(taps, taps2, across, base_copy + 2)
    cot_block = block_of(acts.at[1], 0, mine)
    cot_far = block_of(acts.at[1], 1, mine)
    cot_across = mp_copy(cot_block, cot_far, across, base_copy + 3)
    cot_core = mp_copy(cot_block, cot_block, partner, base_copy + 4)
    cot_pass = mp_copy(cot_far, cot_far, partner, base_copy + 5)
    n1_core = mp_copy(sa.at[mine], sa.at[mine], partner, base_copy + 6)
    n1_far = gm.at[pl.ds(pl.multiple_of(mine * own, own), own)]
    n1_across = mp_copy(sa.at[mine], n1_far, across, base_copy + 7)
    n1_pass = mp_copy(n1_far, n1_far, partner, base_copy + 8)

    def branch_sum(t):
        rows = pl.ds(pl.multiple_of(t * TILE, TILE), TILE)
        number = base_copy + 11 + 2 * per_block + t
        return mp_copy(xr.at[rows], ra.at[0, rows], partner, number)

    n2_block = block_of(acts.at[0], 0, mine)
    n2_core = mp_copy(n2_block, n2_block, partner, base_copy + 10)

    def n2_rows(r, t):
        return acts.at[0, pl.ds(pl.multiple_of(rows_at(r, mine) + t * TILE, TILE), TILE)]

    n2_across = [
        mp_copy(n2_rows(0, t), n2_rows(1, t), across, base_copy + 11 + t) for t in range(per_block)
    ]
    n2_pass = [
        mp_copy(n2_rows(1, t), n2_rows(1, t), partner, base_copy + 11 + per_block + t)
        for t in range(per_block)
    ]

    inw_load.wait()
    for copy in piece_copies:
        copy.start()
    taps[...] = jnp.zeros_like(taps)
    taps[0:3, :] = conv_ref[...].astype(F32)
    taps_copy.start()
    outw_load.wait()
    outw_copy.start()
    cot_load.wait()
    cot_across.start()
    tok_load.wait()

    own_length = lengths[me_mp // 2]

    def own_mask(rows):
        position = lax.broadcasted_iota(jnp.int32, (STRIP, 1), 0) + (core * own + rows.start)
        return (position < own_length).astype(F32)

    def first_norm(rows):
        x_rows = ra[1, rows].astype(F32)
        sa[mine, rows] = (own_mask(rows) * x_rows * rms_scale(x_rows) * gain1[...]).astype(BF16)

    strips(first_norm)
    n1_core.start()
    cot_core.start()

    far = count // 2

    def gather_copy(sub, h, index, number):
        piece = gm.at[piece_rows(lax.rem(index + 2 * count, count)), halves[sub]]
        return ring_copy(piece, piece, sub, h, number)

    for sub in range(2):
        piece_copies[sub].wait_recv()
        for h in range(2):
            gather_copy(sub, h, place, 0).start()

    def gather_hop(hop):
        for sub in range(2):
            for h in range(2):
                arrived = gather_copy(sub, h, place - signs[h] * hop, hop - 1)
                arrived.wait_recv()

                @pl.when(hop < (far if sub == h else far - 1))
                def _():
                    gather_copy(sub, h, place - signs[h] * hop, hop).start()

    def gather_last():
        for h in range(2):
            gather_copy(h, h, place - signs[h] * far, far - 1).wait_recv()
        for number in range(far):
            for sub in range(2):
                for h in range(2):
                    if number < far - 1 or sub == h:
                        gather_copy(sub, h, place, number).wait_send()

    seq_tiles = 2 * per_block

    def project(normed, weights):
        three = dot(normed, weights[0 : 3 * channels], 1, 1)
        return [three[:, k * channels : (k + 1) * channels] for k in range(3)]

    def convolve(mixed, tap_ref):
        mbuf[EDGE:, :] = mixed
        two_back, one_back = mbuf[EDGE - 2 : -2, :], mbuf[EDGE - 1 : -1, :]
        tap = [tap_ref[k : k + 1, :] for k in range(3)]
        conv = tap[0] * two_back + tap[1] * one_back + tap[2] * mixed
        return conv, (two_back, one_back, mixed)

    def carry(mixed):
        mbuf[0:EDGE, :] = mixed[TILE - EDGE :, :]

    def tile_rows(t):
        return pl.ds(pl.multiple_of(t * TILE, TILE), TILE)

    def mixer_tile(weights, tap_ref, at, t):
        normed = sa[t // per_block, tile_rows(lax.rem(t, per_block))]
        left, middle, right = project(normed, weights)
        mixed = left * right
        conv, _ = convolve(mixed, tap_ref)
        carry(mixed)
        aa[tile_rows(t), at * channels : (at + 1) * channels] = (middle * conv).astype(BF16)

    n1_core.wait_recv()
    for item in n1_stores:
        item.start()
    mbuf[0:EDGE, :] = jnp.zeros((EDGE, channels), F32)

    @pl.loop(0, seq_tiles)
    def _(t):
        mixer_tile(wmix, taps, 0, t)

        @pl.when(t + 1 < far)
        def _():
            gather_hop(t + 1)

    assert seq_tiles + 1 >= far
    gather_last()
    taps_copy.wait_recv()
    mbuf[0:EDGE, :] = jnp.zeros((EDGE, channels), F32)

    @pl.loop(0, seq_tiles)
    def _(t):
        mixer_tile(gm, taps2, 1, t)

    outw_copy.wait_recv()

    def branch(c, t):
        rows = pl.ds(pl.multiple_of(c * own + t * TILE, TILE), TILE)
        return dot(aa[rows, 0:channels], outw[...], 1, 0) + dot(
            aa[rows, channels : 2 * channels], outw_far[...], 1, 0
        )

    @pl.loop(0, per_block)
    def _(t):
        xr[pl.ds(pl.multiple_of(t * TILE, TILE), TILE), :] = branch(theirs, t).astype(BF16)
        branch_sum(t).start()

    @pl.loop(0, per_block)
    def _(t):
        f1[pl.ds(pl.multiple_of(t * TILE, TILE), TILE), :] = branch(mine, t)

    first_row = rows_at(0, mine)

    def own_rows(rows):
        return pl.ds(pl.multiple_of(first_row + rows.start, STRIP), STRIP)

    def second_norm(rows):
        hidden = ra[1, rows].astype(F32) + f1[rows] + ra[0, rows].astype(F32)
        f2[rows] = hidden
        acts[0, own_rows(rows)] = (hidden * rms_scale(hidden) * gain2[...]).astype(BF16)

    for t in range(per_block):
        branch_sum(t).wait()

        @pl.loop(0, TILE // STRIP)
        def _(i):
            second_norm(pl.ds(pl.multiple_of(t * TILE + i * STRIP, STRIP), STRIP))

        n2_across[t].start()
    n2_core.start()
    cot_across.wait_recv()
    cot_pass.start()

    def forward_tile(c, start):
        rows = pl.ds(pl.multiple_of(start, TILE), TILE)
        at = pl.multiple_of(c * chunk, chunk)
        both = pl.multiple_of(2 * c * chunk, chunk)
        pre = dot(acts[0, rows], wgu[pl.ds(both, 2 * chunk)], 1, 1)
        grad_activ = dot(acts[1, rows], wd[pl.ds(at, chunk)], 1, 1)
        gate_pre, up_pre = pre[:, :chunk], pre[:, chunk:]
        squash = 0.5 + 0.5 * jnp.tanh(0.5 * gate_pre)
        silu = gate_pre * squash
        aa[rows, pl.ds(at, chunk)] = (silu * up_pre).astype(BF16)
        slope = squash + silu - silu * squash
        agu[rows, pl.ds(both, chunk)] = (grad_activ * up_pre * slope).astype(BF16)
        agu[rows, pl.ds(both + chunk, chunk)] = (grad_activ * silu).astype(BF16)

    def weight_grad(c, part, rows):
        if part < 2:
            cols = pl.ds(pl.multiple_of((2 * c + part) * chunk, chunk), chunk)
            return dot(agu[rows, cols], acts[0, rows], 0, 0)
        return dot(aa[rows, pl.ds(pl.multiple_of(c * chunk, chunk), chunk)], acts[1, rows], 0, 0)

    def weight_grads(c, rows, add):
        def store(into, total):
            if add:
                total = gf[c, into, :].astype(F32) + total
            gf[c, into, :] = total.astype(BF16)

        @pl.loop(0, 2)
        def _(part):
            into = pl.ds(pl.multiple_of(part * chunk, chunk), chunk)
            cols = pl.ds(pl.multiple_of((2 * c + part) * chunk, chunk), chunk)
            store(into, dot(agu[rows, cols], acts[0, rows], 0, 0))

        cols = pl.ds(c * chunk, chunk)
        store(pl.ds(2 * chunk, chunk), dot(aa[rows, cols], acts[1, rows], 0, 0))

    def tile_list(tiles, before):
        def pick(index, at):
            value = jnp.int32(tiles[0][index])
            for i, tile in enumerate(tiles):
                value = jnp.where(at == i, jnp.int32(tile[index]), value)
            return value

        @pl.loop(0, len(tiles))
        def _(at):
            for i, wait in before.items():
                pl.when(at == i)(wait)
            c, r, other, t = (pick(index, at) for index in range(4))
            at_core = mine + other * (theirs - mine)
            forward_tile(c, rows_at(r, at_core) + t * TILE)

    def ready(*items):
        def wait():
            for item in items:
                item.wait()

        return wait

    def near_partner():
        n2_core.wait_recv()
        cot_core.wait_recv()

    def far_own(t):
        def wait():
            n2_across[t].wait_recv()
            n2_pass[t].start()

        return wait

    def far_partner(t):
        def wait():
            n2_pass[t].wait_recv()
            if t == 0:
                cot_pass.wait_recv()

        return wait

    def whole_block(c, r, other):
        return [(c, r, other, t) for t in range(per_block)]

    tile_list(
        whole_block(0, 0, 0) + whole_block(0, 0, 1),
        {0: ready(*weight_loads(0)), per_block: near_partner},
    )
    near, distant = pl.ds(0, 2 * own), pl.ds(2 * own, 2 * own)
    weight_grads(0, near, False)
    order, before = [], {}
    fillers = whole_block(1, 0, 0) + whole_block(1, 0, 1) + whole_block(2, 0, 0)
    fill = len(fillers) // (2 * per_block - 1)
    before[0] = ready(*weight_loads(1))
    for other, t in ((0, 0), (1, 0)) + tuple((o, t) for t in range(1, per_block) for o in (0, 1)):
        taken = fillers[:fill]
        fillers = fillers[fill:]
        for tile in taken:
            if tile[0] == 2 and not any(held[0] == 2 for held in order):
                before[len(order)] = ready(*weight_loads(2))
            order.append(tile)
        before[len(order)] = (far_partner if other else far_own)(t)
        order.append((0, 1, other, t))
    tile_list(order, before)
    n1_across.start()
    weight_grads(0, distant, True)
    sum_start(0)

    def far_tiles(*blocks):
        for block in blocks:
            tile_list(whole_block(*block), {})
            pump()

    def chunk_grads(c):
        weight_grads(c, pl.ds(0, group), False)
        pump()
        sum_start(c)
        pump()

    far_tiles((1, 1, 0), (1, 1, 1))
    chunk_grads(1)
    far_tiles((2, 0, 1), (2, 1, 0), (2, 1, 1))
    for copy in (
        piece_copies
        + n2_across
        + n2_pass
        + [taps_copy, outw_copy, cot_across, cot_core, cot_pass, n1_core, n1_across, n2_core]
    ):
        copy.wait_send()
    for item in n1_stores:
        item.wait()
    def gn2(rows):
        return dot(agu[rows, :], wgu[...], 1, 0)

    def to_send(r):
        def body(rows, local):
            sa[r, local] = gn2(rows).astype(BF16)

        return body

    def to_f1(rows, local):
        f1[local] = gn2(rows)

    core_copies = [mp_copy(sa.at[r], ra.at[r], partner, r) for r in range(2)]
    block_tiles(1, theirs, to_send(1))
    core_copies[1].start()
    pump()
    block_tiles(1, mine, to_f1)
    core_copies[1].wait_recv()

    def join(rows):
        ra[1, rows] = (ra[1, rows].astype(F32) + f1[rows]).astype(BF16)

    strips(join)
    across_copies = []
    for h, number in enumerate((2, base_copy + 12 + 3 * per_block)):
        rows = pl.ds(h * (own // 2), own // 2)
        across_copies.append(mp_copy(ra.at[1, rows], xr.at[rows], across, number))
        across_copies[h].start()
    pump()
    chunk_grads(2)
    pl.semaphore_signal(credit.at[2], inc=1, device_id=across, device_id_type=MESH)
    block_tiles(0, theirs, to_send(0))
    core_copies[0].start()
    pump()
    block_tiles(0, mine, to_f1)
    pump()
    n1_across.wait_recv()
    n1_pass.start()

    pump()
    n1_pass.wait()
    n1_load.start()
    n1_move.start()
    core_copies[0].wait_recv()
    smv[...] = jnp.zeros_like(smv)

    def hidden_grad(rows):
        grad = f1[rows] + ra[0, rows].astype(F32) + xr[rows].astype(F32)
        hidden = f2[rows]
        scale = rms_scale(hidden)
        smv[1:2, :] += jnp.sum(grad * hidden * scale, axis=0, keepdims=True)
        total = acts[1, own_rows(rows)].astype(F32) + rms_back(grad * gain2[...], hidden, scale)
        f1[rows] = total
        acts[1, own_rows(rows)] = total.astype(BF16)

    def block_ref(r, c, h):
        return acts.at[1, pl.ds(pl.multiple_of(rows_at(r, c) + h * (own // 2), STRIP), own // 2)]

    def branch_copy(source, target, device, number):
        return [
            mp_copy(block_ref(*source, h), block_ref(*target, h), device, number[h])
            for h in range(2)
        ]

    more = base_copy + 13 + 3 * per_block
    branch_across = branch_copy((0, mine), (1, mine), across, (3, more))
    branch_core = branch_copy((0, mine), (0, mine), partner, (4, more + 1))
    branch_pass = branch_copy((1, mine), (1, mine), partner, (5, more + 2))
    for h in range(2):
        if h == 1:
            pump()
        across_copies[h].wait_recv()

        @pl.loop(h * (own // 2 // STRIP), (h + 1) * (own // 2 // STRIP))
        def _(t):
            hidden_grad(pl.ds(pl.multiple_of(t * STRIP, STRIP), STRIP))

        if h == 1:
            for copy in core_copies + across_copies:
                copy.wait_send()
        if h == 0:
            pl.semaphore_wait(credit.at[2], 1)
        branch_across[h].start()
        branch_core[h].start()
    pump()

    def out_block(r, c, slot):
        def body(rows, local):
            to = pl.ds(pl.multiple_of(slot * own + local.start, TILE), TILE)
            agu[to, 0:width] = dot(aa[rows, :], wd[...], 1, 0).astype(BF16)

        block_tiles(r, c, body)

    for slot, (r, c) in enumerate(((1, theirs), (0, theirs), (1, mine), (0, mine))):
        out_block(r, c, slot)
        pump()

    for copy in branch_core:
        copy.wait_recv()

    out_copies = [
        mp_copy(agu.at[pl.ds((1 - r) * own, own), pl.ds(0, width)], ra.at[r], partner, 6 + r)
        for r in range(2)
    ]
    for r in (1, 0):
        out_copies[r].start()
    n1_load.wait()
    n1_move.wait()

    def mixer(r):
        def rows_of(t):
            return pl.ds(pl.multiple_of(2 * r * own + t * TILE, TILE), TILE)

        def finish(t):
            tap = [taps[k : k + 1, :] for k in range(3)]
            grad_mixed = (
                tap[2] * gbuf[0:TILE, :]
                + tap[1] * gbuf[1 : TILE + 1, :]
                + tap[0] * gbuf[2 : TILE + 2, :]
            )
            for k, kept in ((0, 1), (2, 0)):
                aa[rows_of(t), k * channels : (k + 1) * channels] = (
                    grad_mixed * pbuf[kept]
                ).astype(BF16)

        mbuf[0:EDGE, :] = jnp.zeros((EDGE, channels), F32)

        @pl.loop(0, seq_tiles)
        def _(t):
            rows = rows_of(t)
            left, middle, right = project(acts[0, rows], wmix)
            mixed = left * right
            conv, shifted = convolve(mixed, taps)
            aa[rows, 3 * channels : 4 * channels] = (middle * conv).astype(BF16)
            grad_mixer = dot(acts[1, rows], outw[...], 1, 1)
            aa[rows, channels : 2 * channels] = (grad_mixer * conv).astype(BF16)
            grad_conv = grad_mixer * middle
            for k, factor in enumerate(shifted):
                smv[2 + k : 3 + k, 0:channels] += jnp.sum(
                    grad_conv * factor, axis=0, keepdims=True
                )
            carry(mixed)

            @pl.when(t > 0)
            def _():
                gbuf[TILE:, :] = grad_conv[0:EDGE, :]
                finish(t - 1)

            gbuf[0:TILE, :] = grad_conv
            pbuf[0] = left
            pbuf[1] = right

        gbuf[TILE:, :] = jnp.zeros((EDGE, channels), F32)
        finish(seq_tiles - 1)

    mixer(0)
    pump()
    pump()

    branch_across[0].wait_recv()
    branch_pass[0].start()
    pump()
    branch_across[1].wait_recv()
    branch_pass[1].start()

    out_copies[1].wait_recv()

    def join_out(rows):
        kept = agu[pl.ds(pl.multiple_of(2 * own + rows.start, STRIP), STRIP), 0:width]
        ra[1, rows] = (ra[1, rows].astype(F32) + kept.astype(F32)).astype(BF16)

    strips(join_out)
    out_across = mp_copy(ra.at[1], xr, across, 8)
    out_across.start()
    pump()
    for copy in branch_pass:
        copy.wait_recv()
    mixer(1)
    pump()

    chunk_end(0)
    for device in (beside, along):
        pl.semaphore_signal(slots_free, inc=1, device_id=device, device_id_type=MESH)

    @pl.when(inside)
    def _():
        pl.semaphore_signal(slots_free, inc=1, device_id=middle, device_id_type=MESH)

    for copy in branch_across + branch_core + branch_pass:
        copy.wait_send()

    for k in range(4):
        used = acts[1] if k == 3 else acts[0]
        cols = slice(k * channels, (k + 1) * channels)
        gm[cols, :] = dot(aa[:, cols], used, 0, 0).astype(BF16)
        pump()
    tok_again.start()

    @pl.when(inside)
    def _():
        pl.semaphore_wait(slots_free, 3)

    @pl.when(jnp.logical_not(inside))
    def _():
        pl.semaphore_wait(slots_free, 2)

    sum_start(CHUNKS)

    def gn1(rows):
        return dot(aa[rows, 0 : 3 * channels], inw[...], 1, 0)

    def to_stage(r):
        def body(rows, local):
            to = pl.ds(pl.multiple_of(r * own + local.start, TILE), TILE)
            agu[to, width : 2 * width] = gn1(rows).astype(BF16)

        return body

    def to_f2(rows, local):
        f2[local] = gn1(rows)

    back_copies = [
        mp_copy(agu.at[pl.ds(r * own, own), pl.ds(width, width)], ra.at[r], partner, 9 + r)
        for r in range(2)
    ]
    for r in (1, 0):
        block_tiles(r, theirs, to_stage(r))
        pump()
    pump()

    out_copies[0].wait_recv()
    out_across.wait_recv()

    def finish_out(rows):
        kept = agu[pl.ds(pl.multiple_of(3 * own + rows.start, STRIP), STRIP), 0:width]
        total = f2[rows] + kept.astype(F32) + ra[0, rows].astype(F32) + xr[rows].astype(F32)
        sa[0, rows] = total.astype(BF16)

    strips(finish_out)
    out_store.start()
    for copy in out_copies + [out_across]:
        copy.wait_send()
    pl.semaphore_signal(credit.at[0], inc=1, device_id=partner, device_id_type=MESH)
    pl.semaphore_signal(credit.at[1], inc=1, device_id=across, device_id_type=MESH)

    pump()
    pl.semaphore_wait(credit.at[0], 1)
    pl.semaphore_wait(credit.at[1], 1)
    for r in (1, 0):
        back_copies[r].start()
    block_tiles(1, mine, to_f2)
    pump()
    pump()
    back_copies[1].wait_recv()

    def join_back(rows):
        ra[1, rows] = (ra[1, rows].astype(F32) + f2[rows]).astype(BF16)

    strips(join_back)
    back_across = mp_copy(ra.at[1], xr, across, 11)
    back_across.start()
    block_tiles(0, mine, to_f2)
    pump()
    pump()
    back_copies[0].wait_recv()
    back_across.wait_recv()

    def tokens_grad(rows):
        grad = f2[rows] + ra[0, rows].astype(F32) + xr[rows].astype(F32)
        grad = grad * own_mask(rows)
        x_rows = acts[0, rows].astype(F32)
        scale = rms_scale(x_rows)
        smv[0:1, :] += jnp.sum(grad * x_rows * scale, axis=0, keepdims=True)
        total = f1[rows] + rms_back(grad * gain1[...], x_rows, scale)
        sa[1, rows] = total.astype(BF16)

    tok_again.wait()
    strips(tokens_grad)
    tg_store.start()
    chunk_end(1)
    for copy in back_copies + [back_across]:
        copy.wait_send()

    small_core = mp_copy(smv, smb.at[0], partner, 12)
    small_core.start()
    pump()
    small_core.wait()
    smv[0:2, :] += smb[0, 0:2]
    small_across = mp_copy(smv, smb.at[1], across, 13)
    small_across.start()
    pump()
    small_across.wait()
    smv[0:2, :] += smb[1, 0:2]
    for hop, device in enumerate((beside, along, opposite)):
        swap = mp_copy(smv, smb.at[2 + hop], device, 14 + hop)
        swap.start()
        pump()
        swap.wait()
        smv[...] += smb[2 + hop]
    small_out[...] = smv[...]
    chunk_end(2)
    pump()
    assert next(sites, None) is None
    for number in range(CUT * CHUNKS, len(parts_list)):
        parts_list[number][2]()
    for item in mixer_stores:
        item.start()
    for item in grad_stores + mixer_stores:
        item.wait()
    out_store.wait()
    tg_store.wait()


def block_by_kernel(
    tokens,
    lengths,
    norm1_gain,
    in_weight,
    conv_weight,
    out_weight,
    norm2_gain,
    gate_weight,
    up_weight,
    down_weight,
    cotangent,
):
    count = lax.axis_size("dp")
    own, width = tokens.shape
    group = 4 * own
    channels = out_weight.shape[0]
    units = gate_weight.shape[0]
    chunk = units // CHUNKS
    part_rows, first = 3 * chunk // CUT, 5 * width // 8
    mp_copies = 14 + count - 1 + 16 + 3 * (own // TILE)
    anywhere = pl.BlockSpec(memory_space=pl.ANY)
    inside = pl.BlockSpec(memory_space=pltpu.VMEM)
    macs = group * width * (3 * 3 * units + 15 * channels)
    outs = pl.pallas_call(
        functools.partial(block_kernel, count),
        out_shape=(
            jax.ShapeDtypeStruct((own, width), BF16),
            jax.ShapeDtypeStruct((own, width), BF16),
            jax.ShapeDtypeStruct((units, width), BF16),
            jax.ShapeDtypeStruct((units, width), BF16),
            jax.ShapeDtypeStruct((units, width), BF16),
            jax.ShapeDtypeStruct((3 * channels, width), BF16),
            jax.ShapeDtypeStruct((channels, width), BF16),
            jax.ShapeDtypeStruct((8, width), F32),
            jax.ShapeDtypeStruct((2 * own, width), BF16),
        ),
        in_specs=[anywhere] * 7 + [inside] * 3 + [pl.BlockSpec(memory_space=pltpu.SMEM)],
        out_specs=(anywhere,) * 7 + (inside, anywhere),
        scratch_shapes=[
            pltpu.VMEM((2, group, width), BF16),
            pltpu.VMEM((2 * units, width), BF16),
            pltpu.VMEM((units, width), BF16),
            pltpu.VMEM((group, 2 * units), BF16),
            pltpu.VMEM((group, units), BF16),
            pltpu.VMEM((CHUNKS, 3 * chunk, width), BF16),
            pltpu.VMEM((CUT * CHUNKS, part_rows // 2, first), BF16),
            pltpu.VMEM((CUT * CHUNKS, 2, part_rows // 4, first), BF16),
            pltpu.VMEM((CUT * CHUNKS, 2, part_rows // 2, width - first), BF16),
            pltpu.VMEM((4 * channels, width), BF16),
            pltpu.VMEM((2, own, width), BF16),
            pltpu.VMEM((2, own, width), BF16),
            pltpu.VMEM((own, width), BF16),
            pltpu.VMEM((4 * channels, width), BF16),
            pltpu.VMEM((own, width), F32),
            pltpu.VMEM((own, width), F32),
            pltpu.VMEM((8, channels), F32),
            pltpu.VMEM((8, channels), F32),
            pltpu.VMEM((EDGE + TILE, channels), F32),
            pltpu.VMEM((TILE + EDGE, channels), F32),
            pltpu.VMEM((2, TILE, channels), F32),
            pltpu.VMEM((8, width), F32),
            pltpu.VMEM((5, 8, width), F32),
            pltpu.SemaphoreType.DMA((3 * CHUNKS + 10 + 3 * CHUNKS + 2,)),
            pltpu.SemaphoreType.DMA((2, 2, count // 2)),
            pltpu.SemaphoreType.DMA((2, 2, count // 2)),
            pltpu.SemaphoreType.DMA((CUT * CHUNKS + SLABS, 11)),
            pltpu.SemaphoreType.DMA((CUT * CHUNKS + SLABS, 11)),
            pltpu.SemaphoreType.REGULAR((CUT * CHUNKS + SLABS,)),
            pltpu.SemaphoreType.REGULAR((CUT * CHUNKS + SLABS,)),
            pltpu.SemaphoreType.REGULAR,
            pltpu.SemaphoreType.DMA((mp_copies,)),
            pltpu.SemaphoreType.DMA((mp_copies,)),
            pltpu.SemaphoreType.REGULAR((3,)),
        ],
        compiler_params=pltpu.CompilerParams(
            collective_id=0, has_side_effects=True, vmem_limit_bytes=VMEM_BYTES
        ),
        cost_estimate=pl.CostEstimate(
            flops=2 * macs, bytes_accessed=64 * 2**20, transcendentals=group * units
        ),
        name="block",
    )(
        tokens,
        cotangent,
        gate_weight,
        up_weight,
        down_weight,
        in_weight.reshape(3 * channels, width),
        out_weight,
        conv_weight,
        norm1_gain.reshape(1, width),
        norm2_gain.reshape(1, width),
        lengths,
    )
    held = 2 * own + 3 * units + 4 * channels
    finals = pl.pallas_call(
        widen_kernel,
        out_shape=(
            jax.ShapeDtypeStruct((own, width), BF16),
            jax.ShapeDtypeStruct((own, width), BF16),
            jax.ShapeDtypeStruct((units, width), F32),
            jax.ShapeDtypeStruct((units, width), F32),
            jax.ShapeDtypeStruct((units, width), F32),
            jax.ShapeDtypeStruct((3 * channels, width), F32),
            jax.ShapeDtypeStruct((channels, width), F32),
            jax.ShapeDtypeStruct((1, width), F32),
            jax.ShapeDtypeStruct((1, width), F32),
            jax.ShapeDtypeStruct((3, channels), F32),
        ),
        in_specs=[anywhere] * 7 + [inside],
        out_specs=(anywhere,) * 7 + (inside,) * 3,
        scratch_shapes=[
            pltpu.VMEM((held, width), BF16),
            pltpu.VMEM((held, width), F32),
            pltpu.SemaphoreType.DMA((2 * held // LANES,)),
        ],
        compiler_params=pltpu.CompilerParams(vmem_limit_bytes=WIDEN_BYTES),
        cost_estimate=pl.CostEstimate(flops=0, bytes_accessed=32 * 2**20, transcendentals=0),
        name="widen",
    )(*outs[:8])
    result, grad_tokens, gate_grad, up_grad, down_grad, in_grad, out_grad, one, two, taps = finals
    return (
        result,
        grad_tokens,
        one.reshape(width),
        in_grad.reshape(3, channels, width),
        taps,
        out_grad,
        two.reshape(width),
        gate_grad,
        up_grad,
        down_grad,
    )


def widen_kernel(*refs):
    sources, small = refs[:7], refs[7]
    targets, one, two, taps = refs[8:15], refs[15], refs[16], refs[17]
    narrow, wide, sem = refs[18:]
    reads, writes = [], []
    at = 0
    for i, (source, target) in enumerate(zip(sources, targets)):
        for row in range(0, source.shape[0], LANES):
            rows, held = pl.ds(row, LANES), pl.ds(at, LANES)
            number = 2 * (at // LANES)
            reads.append(pltpu.make_async_copy(source.at[rows], narrow.at[held], sem.at[number]))
            out = (narrow if i < 2 else wide).at[held]
            writes.append(pltpu.make_async_copy(out, target.at[rows], sem.at[number + 1]))
            at += LANES
    passed = 2 * sources[0].shape[0] // LANES
    for copy in reads:
        copy.start()
    one[...] = small[0:1, :]
    two[...] = small[1:2, :]
    taps[...] = small[2:5, : taps.shape[1]]
    for i, (read, write) in enumerate(zip(reads, writes)):
        read.wait()
        if i >= passed:
            rows = slice(i * LANES, (i + 1) * LANES)
            wide[rows, :] = narrow[rows, :].astype(F32)
        write.start()
    for copy in writes:
        copy.wait()


VMEM_BYTES = 62 * 2**20
WIDEN_BYTES = 62 * 2**20


def on_device(
    tokens,
    lengths,
    norm1_gain,
    in_weight,
    conv_weight,
    out_weight,
    norm2_gain,
    gate_weight,
    up_weight,
    down_weight,
    cotangent,
):
    assert 2 * tokens.shape[0] == SEQ_LEN
    fits = lax.axis_size("mp") == 4 and lax.axis_size("dp") == 8
    block = block_by_kernel if fits else block_by_ops
    return block(
        tokens,
        lengths,
        norm1_gain,
        in_weight,
        conv_weight,
        out_weight,
        norm2_gain,
        gate_weight,
        up_weight,
        down_weight,
        cotangent,
    )


def solution(mesh):
    rows = P(("dp", "mp"), None)
    hidden_rows = P("mp", None)
    placed = (
        rows,
        P("dp"),
        P(),
        P(None, "mp", None),
        P(None, "mp"),
        hidden_rows,
        P(),
        hidden_rows,
        hidden_rows,
        hidden_rows,
        rows,
    )
    return jax.shard_map(
        on_device,
        mesh=mesh,
        in_specs=placed,
        out_specs=(
            rows,
            rows,
            P(),
            P(None, "mp", None),
            P(None, "mp"),
            hidden_rows,
            P(),
            hidden_rows,
            hidden_rows,
            hidden_rows,
        ),
        check_vma=False,
    )
```

time: 871 us -> 264 us (0.30)
  waiting for transfers between devices: 583 us -> 0 us
  Pallas kernels: 0 us -> 263 us
  matrix products: 150 us -> 0 us
  blocking collectives: 63 us -> 0 us
  other arithmetic: 47.3 us -> 0 us
  between operations: 14.8 us -> 0.84 us
    pallas_call x0 -> x2, Pallas kernels: none -> 263 us  [the longest x1 251 us: block_by_kernel(): pl.pallas_call(functools.partial(block_kernel, count), out_shape=(jax.Sha...]
    reduce_scatter x5 -> x0, waiting for transfers between devices: 209 us -> none  [the longest x2 88.3 us: split_forward(): lax.psum_scatter(lax.dot_general(col_block, out_weight, CONTRACT_ROWS, pr...]
    psum x1 -> x0, waiting for transfers between devices: 208 us -> none  [on_device(): lax.psum(weight_parts[0].astype(jnp.bfloat16), 'dp').astype(jnp.float32)]
    all_gather x6 -> x0, waiting for transfers between devices: 165 us -> none  [the longest x2 71.8 us: split_forward(): normed_one_all = lax.all_gather(normed_one, 'mp', axis=0, tiled=True)]
    dot_general x18 -> x0, matrix products: 150 us -> none  [the longest x2 30.3 us: split_forward(): jnp.einsum('fi,ti->ft', gate_weight, normed_two_all, preferred_element_ty...]
    psum x2 -> x0, blocking collectives: 63 us -> none  [the longest x1 40.1 us: on_device(): gain_sums = lax.psum((gain_parts[0], gain_parts[1]), ('dp', 'mp'))]
    convert_element_type x15 -> x0, other arithmetic: 30.3 us -> none  [the longest x1 3.97 us: split_backward(): grad_tokens.astype(jnp.bfloat16)]
    reduce_sum x7 -> x0, other arithmetic: 11 us -> none  [the longest x4 5.39 us: rms_scale(): jnp.mean(row_data * row_data, axis=-1, keepdims=True) + NORM_EPS]
  transfers between devices with their start and end apart: 12 -> 0, of which waited for: 11 -> 0; matrix products, arithmetic and copies ran while one was open for 11% -> 0% of each run, Pallas kernels for 0% -> 0%
where the time goes in v1:
time: 264 us
  Pallas kernels  263 us (100%)
    pallas_call x1, Pallas kernels, block_by_kernel(): pl.pallas_call(functools.partial(block_kernel, count), out_shape=(jax.Sha...  251 us
    pallas_call x1, Pallas kernels, block_by_kernel(): pl.pallas_call(widen_kernel, out_shape=(jax.ShapeDtypeStruct((own, width)...  12.6 us

profile of v1, /device:TPU:0, one launch (start us, length us, event | category | flops | bytes accessed | tf_op | source)
XLA Modules:
  0.0 264.1 jit_solution(6300573869986081114)
XLA Ops:
  0.6 250.6 %block.1 = (bf16[512,1024]{1,0:T(8,128)(2,1)}, bf16[512,1024]{1,0:T(8,128)(2,1)}, bf16[1152,1024]{1,0:T(8,128)(2,1)}, bf16[1152,1024]{1,0:T(8,128)(2,1)}, bf16[1...) custom-call(bf16[512,1024]{1,0:T(8,128)(2,1)} %tok_hbm.1, ...), custom_call_target="tpu_custom_call" | custom-call | flops 59592671232 | bytes 67108864 | tf_op jit(solution)/shard_map/block/pallas_call | solution.py:1367
  251.3 12.6 %widen.1 = (bf16[512,1024]{1,0:T(8,128)(2,1)}, bf16[512,1024]{1,0:T(8,128)(2,1)}, f32[1152,1024]{1,0:T(8,128)}, f32[1152,1024]{1,0:T(8,128)}, f32[1152,1024]{1,0...) custom-call(bf16[512,1024]{1,0:T(8,128)(2,1)} %get-tuple-element.28., ...), custom_call_target="tpu_custom_call" | custom-call | bytes 33554432 | tf_op jit(solution)/shard_map/widen/pallas_call | solution.py:1439

commit v2 on v1

--- a/solution.py
+++ b/solution.py
@@ -245,90 +245,93 @@
     (),
     (),
     (0,),
+    (),
+    (),
+    (),
     (100,),
-    (),
-    (9,),
-    (200,),
-    (109, 300),
-    (3, 10),
-    (110, 209),
-    (),
-    (309, 103),
-    (210, 203),
-    (),
-    (),
-    (303, 400, 6),
-    (),
-    (500, 13),
+    (9, 200),
+    (109, 300, 3),
+    (10, 209, 110, 309),
+    (),
+    (),
+    (103, 210),
+    (),
+    (),
+    (203,),
+    (),
+    (),
+    (303,),
+    (400, 500, 409, 13),
     (310,),
-    (113,),
-    (409, 509),
-    (),
-    (),
-    (106,),
-    (410, 213, 510),
-    (206,),
-    (),
-    (306,),
-    (),
-    (403,),
-    (),
-    (),
-    (600, 503),
-    (313,),
-    (700,),
-    (800, 413),
-    (900, 513, 609, 709, 809, 610, 909, 710, 603, 810, 406, 910, 703),
-    (803, 903, 506, 613),
+    (),
+    (),
+    (509, 106, 410),
+    (6, 510, 206, 113),
+    (),
+    (),
+    (),
+    (),
+    (),
+    (600,),
+    (403, 213),
+    (),
+    (),
+    (503, 700),
+    (900, 609, 800, 709, 809, 909, 513, 306, 413),
+    (610, 710, 810, 603, 910, 313, 703, 506, 803),
+    (903, 406),
+    (606,),
     (),
     (713,),
-    (),
-    (606,),
-    (813, 913, 706, 806, 906),
+    (613, 706, 806, 906),
+    (913, 813),
 )
 INSIDE = (
     (),
     (7,),
-    (0, 107, 8, 100),
-    (),
-    (1,),
+    (107,),
+    (),
+    (8, 0, 1),
     (108, 207),
-    (200, 2, 307),
-    (208, 101, 300, 201),
-    (308, 301, 102),
-    (4, 202, 11, 302),
-    (111,),
-    (5, 407),
-    (12, 507),
-    (),
-    (),
-    (400, 112, 104, 408),
-    (211, 500, 204),
-    (508,),
-    (304, 105),
-    (401,),
-    (212, 501, 205, 311),
-    (),
-    (),
-    (305, 402),
-    (502, 312, 411),
-    (),
-    (),
-    (511,),
+    (2, 307, 100, 200, 208, 101),
+    (308, 201, 300),
+    (301, 102, 202, 4),
+    (),
+    (5, 11),
+    (111, 302),
+    (407,),
+    (12,),
+    (507, 112),
+    (400, 104, 408),
+    (),
+    (),
+    (508, 211),
+    (204, 105),
+    (304,),
+    (212, 401),
+    (205,),
+    (500, 501, 305, 311, 402),
+    (502, 411),
+    (),
+    (312, 511),
     (412,),
-    (607, 707),
-    (807, 600, 512),
-    (),
-    (907, 608, 700, 708),
-    (808, 601, 800, 908),
-    (404,),
-    (900, 602, 701, 504),
-    (801, 405, 901, 702, 505, 611, 802, 711, 902, 604, 612, 811, 712, 911, 605, 704, 812),
-    (912, 705, 804, 904),
-    (),
-    (),
-    (805,),
-    (905,),
+    (),
+    (807, 607),
+    (707, 512),
+    (),
+    (),
+    (907, 608, 404, 600, 808, 708, 700),
+    (601,),
+    (908, 504),
+    (
+        900, 701, 405, 800, 901, 602, 801, 505, 702, 611, 802, 711, 902, 811, 612, 604, 812,
+        911, 605, 704, 712,
+    ),
+    (804, 912, 904, 705),
+    (805, 905),
+    (),
+    (),
+    (),
     (),
 )
 CUT = 2
@@ -465,10 +468,12 @@
         for c in range(CHUNKS)
     ]
     late += 3 * CHUNKS
-    mixer_stores = [
-        load(gm.at[pl.ds(0, 3 * channels)], in_out, late),
-        load(gm.at[pl.ds(3 * channels, channels)], mix_out, late + 1),
-    ]
+    slab_rows = 4 * channels // SLABS
+    mixer_stores = []
+    for k in range(SLABS):
+        target = mix_out if k == SLABS - 1 else in_out.at[pl.ds(k * slab_rows, slab_rows)]
+        mixer_stores.append(load(gm.at[pl.ds(k * slab_rows, slab_rows)], target, late + k))
+    assert slab_rows == channels
 
     for item in (inw_load, outw_load, cot_load, tok_load):
         item.start()
@@ -639,7 +644,7 @@
 
         return begin, sum_rows, end
 
-    part_rows, slab_rows = 3 * chunk // CUT, 4 * channels // SLABS
+    part_rows = 3 * chunk // CUT
     parts_list = []
     for c in range(CHUNKS):
         for k in range(CUT):
@@ -1332,8 +1337,7 @@
     assert next(sites, None) is None
     for number in range(CUT * CHUNKS, len(parts_list)):
         parts_list[number][2]()
-    for item in mixer_stores:
-        item.start()
+        mixer_stores[number - CUT * CHUNKS].start()
     for item in grad_stores + mixer_stores:
         item.wait()
     out_store.wait()
@@ -1403,7 +1407,7 @@
             pltpu.VMEM((2, TILE, channels), F32),
             pltpu.VMEM((8, width), F32),
             pltpu.VMEM((5, 8, width), F32),
-            pltpu.SemaphoreType.DMA((3 * CHUNKS + 10 + 3 * CHUNKS + 2,)),
+            pltpu.SemaphoreType.DMA((3 * CHUNKS + 10 + 3 * CHUNKS + SLABS,)),
             pltpu.SemaphoreType.DMA((2, 2, count // 2)),
             pltpu.SemaphoreType.DMA((2, 2, count // 2)),
             pltpu.SemaphoreType.DMA((CUT * CHUNKS + SLABS, 11)),
@@ -1480,34 +1484,36 @@
     sources, small = refs[:7], refs[7]
     targets, one, two, taps = refs[8:15], refs[15], refs[16], refs[17]
     narrow, wide, sem = refs[18:]
-    reads, writes = [], []
+    moves = []
     at = 0
     for i, (source, target) in enumerate(zip(sources, targets)):
-        for row in range(0, source.shape[0], LANES):
-            rows, held = pl.ds(row, LANES), pl.ds(at, LANES)
-            number = 2 * (at // LANES)
-            reads.append(pltpu.make_async_copy(source.at[rows], narrow.at[held], sem.at[number]))
+        rows = source.shape[0]
+        if rows % WIDEN_ROWS == 0:
+            rows = WIDEN_ROWS
+        for row in range(0, source.shape[0], rows):
+            place, held = pl.ds(row, rows), pl.ds(at, rows)
+            number = 2 * len(moves)
+            read = pltpu.make_async_copy(source.at[place], narrow.at[held], sem.at[number])
             out = (narrow if i < 2 else wide).at[held]
-            writes.append(pltpu.make_async_copy(out, target.at[rows], sem.at[number + 1]))
-            at += LANES
-    passed = 2 * sources[0].shape[0] // LANES
-    for copy in reads:
-        copy.start()
+            write = pltpu.make_async_copy(out, target.at[place], sem.at[number + 1])
+            read.start()
+            moves.append((read, write, held, i >= 2))
+            at += rows
     one[...] = small[0:1, :]
     two[...] = small[1:2, :]
     taps[...] = small[2:5, : taps.shape[1]]
-    for i, (read, write) in enumerate(zip(reads, writes)):
+    for read, write, held, widens in moves:
         read.wait()
-        if i >= passed:
-            rows = slice(i * LANES, (i + 1) * LANES)
-            wide[rows, :] = narrow[rows, :].astype(F32)
+        if widens:
+            wide[held, :] = narrow[held, :].astype(F32)
         write.start()
-    for copy in writes:
-        copy.wait()
+    for _, write, _, _ in moves:
+        write.wait()
 
 
 VMEM_BYTES = 62 * 2**20
 WIDEN_BYTES = 62 * 2**20
+WIDEN_ROWS = 384
 
 
 def on_device(

time: 264 us -> 263 us (level)
  no operation moved by 1% of the time
where the time goes in v2:
time: 263 us
  Pallas kernels  262 us (100%)
    pallas_call x1, Pallas kernels, block_by_kernel(): pl.pallas_call(functools.partial(block_kernel, count), out_shape=(jax.Sha...  250 us
    pallas_call x1, Pallas kernels, block_by_kernel(): pl.pallas_call(widen_kernel, out_shape=(jax.ShapeDtypeStruct((own, width)...  12.3 us

profile of v2, /device:TPU:0, one launch (start us, length us, event | category | flops | bytes accessed | tf_op | source)
XLA Modules:
  0.0 263.2 jit_solution(14436236379400583903)
XLA Ops:
  0.6 250.0 %block.1 = (bf16[512,1024]{1,0:T(8,128)(2,1)}, bf16[512,1024]{1,0:T(8,128)(2,1)}, bf16[1152,1024]{1,0:T(8,128)(2,1)}, bf16[1152,1024]{1,0:T(8,128)(2,1)}, bf16[1...) custom-call(bf16[512,1024]{1,0:T(8,128)(2,1)} %tok_hbm.1, ...), custom_call_target="tpu_custom_call" | custom-call | flops 59592671232 | bytes 67108864 | tf_op jit(solution)/shard_map/block/pallas_call | solution.py:1371
  250.7 12.3 %widen.1 = (bf16[512,1024]{1,0:T(8,128)(2,1)}, bf16[512,1024]{1,0:T(8,128)(2,1)}, f32[1152,1024]{1,0:T(8,128)}, f32[1152,1024]{1,0:T(8,128)}, f32[1152,1024]{1,0...) custom-call(bf16[512,1024]{1,0:T(8,128)(2,1)} %get-tuple-element.28., ...), custom_call_target="tpu_custom_call" | custom-call | bytes 33554432 | tf_op jit(solution)/shard_map/widen/pallas_call | solution.py:1443
